TPU v7x, 32 devices: a whole 2x2x4 slice. The times are simulated.
32 devices in a mesh: chan: 32 (over z, y, x, core).
Axes of the slice: x: 2, y: 2, z: 4, core: 2. Of those that a mesh axis runs over, the one named last changes fastest.
Arguments:
- tokens: bfloat16 [11328, 768], P('chan'), may hold values from -6 to 6
- row_pixel: int32 [11328], replicated, may hold values from 0 to 11327, each once
- coef_height: float32 [768, 64], P('chan'), may hold values from -0.75 to 0.75
- rate_height: float32 [768, 64], P('chan'), may hold values from -1 to 2.5
- coef_width: float32 [768, 64], P('chan'), may hold values from -0.75 to 0.75
- rate_width: float32 [768, 64], P('chan'), may hold values from -1 to 2.5
- skip_weight: float32 [768], P('chan'), may hold values from 0.5 to 1.5
- norm_gain: float32 [768], replicated, may hold values from 0.5 to 1.5
- norm_bias: float32 [768], replicated, may hold values from -4 to 4
- weight_in: bfloat16 [768, 3072], replicated, may hold values from -0.21875 to 0.21875
- bias_in: float32 [3072], replicated, may hold values from -4 to 4
- weight_out: bfloat16 [3072, 768], replicated, may hold values from -0.109375 to 0.109375
- bias_out: float32 [768], replicated, may hold values from -4 to 4
- layer_scale: float32 [768], replicated, may hold values from 0.5 to 1.5
- out_grad: bfloat16 [11328, 768], P('chan'), may hold values from -6 to 6
Outputs:
- block_out: bfloat16 [11328, 768], P('chan')
- grad_tokens: float32 [11328, 768], P('chan')
- grad_coef_height: float32 [768, 64], P('chan')
- grad_rate_height: float32 [768, 64], P('chan')
- grad_coef_width: float32 [768, 64], P('chan')
- grad_rate_width: float32 [768, 64], P('chan')
- grad_skip_weight: float32 [768], P('chan')
- grad_norm_gain: float32 [768], P('chan')
- grad_norm_bias: float32 [768], P('chan')
- grad_weight_in: float32 [768, 3072], P('chan')
- grad_bias_in: float32 [3072], P('chan')
- grad_weight_out: float32 [3072, 768], P('chan')
- grad_bias_out: float32 [768], P('chan')
- grad_layer_scale: float32 [768], P('chan')
Inputs may be any that keep to these rules, and one draw needn't show every extreme that they name: Row r of the block holds pixel row_pixel[r] of the image order; every pixel is held by exactly one row.
All inputs are finite; a program needn't handle non-finite values.
Results may differ from a plain program's by a relative error of at most 0.0073.
Values may be sent and summed in bfloat16 or wider, within the bound.
No kernel may reach another device: no remote copies, remote signals or barrier semaphores. Data moves between devices by JAX's collectives and lax.ppermute only.
A program may use at most 320 MiB of HBM per device.

v0:
```python
import functools
import math

import jax
import jax.numpy as jnp
import numpy as np
from jax import lax
from jax.experimental import pallas as pl
from jax.experimental.pallas import tpu as pltpu
from jax.sharding import PartitionSpec as P

SIDES = (10, 14, 18)
SHARES = (1, 1, 2)
UNIT = sum(m * s * s for s, m in zip(SIDES, SHARES))
TAPS = sum(SIDES)
EPSILON = 1e-06
LANES = 128
SUB = 8
MARGIN = 32
VMEM = 63 * 2**20
LESS = 36 * 2**20
SMALL = 20 * 2**20
CHUNKS = 3
F32 = jnp.float32
BF16 = jnp.bfloat16


class Plan:
    def __init__(self, devices, rows, channels):
        self.devices, self.rows, self.channels = devices, rows, channels
        self.pixels = devices * rows
        self.units = self.pixels // UNIT
        self.slots = LANES // channels
        self.row_pad = -(-rows // LANES) * LANES
        self.extra_row = -(-rows // SUB) * SUB
        self.sections = []
        image_row, packed_row, tap, mask_row, pixel = 0, 0, 0, 0, 0
        for side, share in zip(SIDES, SHARES):
            images = share * self.units
            pitch = -(-side // SUB) * SUB
            groups = -(-images // self.slots)
            self.sections.append(
                dict(side=side, images=images, pitch=pitch, groups=groups, image_row=image_row, packed_row=packed_row, tap=tap, mask_row=mask_row, pixel=pixel)
            )
            image_row += groups * self.slots * side * pitch
            packed_row += groups * side * pitch
            tap += side
            mask_row += side * pitch
            pixel += images * side * side
        self.image_rows = image_row
        self.packed_rows = packed_row
        self.mask_rows = mask_row

    @property
    def extra_lane(self):
        return self.extra_row - (self.row_pad - LANES)

    def kind(self, lane, which):
        return (lane == self.extra_lane + which) | (lane == self.extra_lane + SUB + which)

    def fits(self):
        room = self.row_pad - self.extra_row >= 2 * SUB
        return room and self.channels % SUB == 0 and 4 * LANES * (self.image_rows + 2 * self.row_pad + 5 * self.packed_rows) < 40 * 2**20

    def address(self, row_pixel):
        where = jnp.zeros_like(row_pixel)
        for part in self.sections:
            local = row_pixel - part["pixel"]
            line = local // part["side"]
            spot = part["image_row"] + line * part["pitch"] + local - line * part["side"]
            where = jnp.where(local >= 0, spot, where)
        return where

    def spread(self):
        lane = np.arange(LANES)
        held = (lane[None, :] % self.channels == np.arange(self.channels)[:, None]) & (lane[None, :] < self.slots * self.channels)
        return jnp.asarray(held.astype(np.float32), BF16)

    def tile_taps(self, taps):
        tiled = jnp.tile(taps, (1, self.slots))
        return jnp.pad(tiled, ((0, 0), (0, LANES - tiled.shape[1])))


def slot_masks(plan):
    lane = lax.broadcasted_iota(jnp.int32, (SUB, LANES), 1)
    return [(lane >= q * plan.channels) & (lane < (q + 1) * plan.channels) for q in range(plan.slots)]


def in_turn(plan, first, second, beside=None, steps=0, ready=None):
    first(0, 0)

    def pair(k):
        first(2 * k + 1, 1)
        second(2 * k, 0)
        first(2 * k + 2, 0)
        second(2 * k + 1, 1)

    def plain(k, carry):
        pair(k)
        return carry

    def more(k, carry):
        beside(k - begin)
        pair(k)
        return carry

    pairs = plan.devices // 2 - 1
    begin = pairs - steps
    lax.fori_loop(0, begin, plain, 0)
    if steps:
        ready()
        lax.fori_loop(begin, pairs, more, 0)
    first(plan.devices - 1, 1)
    second(plan.devices - 2, 0)
    second(plan.devices - 1, 1)


def scatter_rows(plan, where, block, buffers, image, beside=None, steps=0, ready=None):
    def turn(s, held):
        rows = block[s].astype(F32)
        full = [rows] * plan.slots
        if LANES > plan.slots * plan.channels:
            full.append(rows[: LANES - plan.slots * plan.channels])
        buffers[held][pl.ds(0, plan.rows), :] = jnp.concatenate(full, axis=0).T

    def place(s, held):
        base = s * plan.rows
        for u in range(plan.rows):
            image[pl.ds(where[base + u], 1), :] = buffers[held][pl.ds(u, 1), :]

    in_turn(plan, turn, place, beside, steps, ready)


def gather_rows(plan, where, buffers, image, out, extra=None, leave=None):
    def fetch(s, held):
        base = s * plan.rows
        for u in range(plan.rows):
            buffers[held][pl.ds(u, 1), :] = image[pl.ds(where[base + u], 1), :]

    def fold(s, held):
        turned = buffers[held][...].T
        folded = turned[: plan.channels]
        for q in range(1, plan.slots):
            folded = folded + turned[q * plan.channels : (q + 1) * plan.channels]
        if extra is None:
            out[s] = folded[:, : plan.rows].astype(BF16)
            leave(s)
            return
        last = plan.row_pad - LANES
        sums = extra[pl.ds(pl.multiple_of(s * plan.channels, SUB), plan.channels), :]
        lane = lax.broadcasted_iota(jnp.int32, sums.shape, 1) + last
        out[s, :, pl.ds(0, last)] = folded[:, :last].astype(BF16)
        out[s, :, pl.ds(last, LANES)] = jnp.where(lane < plan.extra_row, folded[:, last:], sums).astype(BF16)

    in_turn(plan, fetch, fold)


def pack_images(plan, masks, image, packed, margin):
    place = lax.broadcasted_iota(jnp.int32, (SUB, LANES), 0)
    for part in plan.sections:
        side, pitch = part["side"], part["pitch"]
        area = side * pitch
        ragged = part["images"] < part["groups"] * plan.slots

        def group(t, carry, part=part, side=side, pitch=pitch, area=area, ragged=ragged):
            start = part["image_row"] + t * (plan.slots * area)
            target = margin + part["packed_row"] + t * area
            used = masks
            if ragged:
                used = [mask & (t * plan.slots + q < part["images"]) for q, mask in enumerate(masks)]
            ends = [mask & (place < side % SUB) for mask in used]
            for i in range(side):
                for j in range(0, pitch, SUB):
                    value = jnp.zeros((SUB, LANES), F32)
                    for q in range(plan.slots):
                        row = pl.multiple_of(start + (q * area + i * pitch + j), SUB)
                        value = jnp.where((ends if j + SUB > side else used)[q], image[pl.ds(row, SUB), :], value)
                    packed[pl.ds(pl.multiple_of(target + (i * pitch + j), SUB), SUB), :] = value
            return carry

        lax.fori_loop(0, part["groups"], group, 0)


def unpack_line(plan, masks, part, t, offset, value, image):
    area = part["side"] * part["pitch"]
    for q in range(plan.slots):
        row = pl.multiple_of(part["image_row"] + (t * plan.slots + q) * area + offset, SUB)
        image[pl.ds(row, SUB), :] = jnp.where(masks[q], value, 0.0)


def wide_taps(plan, taps, table):
    for tap in range(TAPS):
        table[pl.ds(tap * SUB, SUB), :] = jnp.broadcast_to(taps[pl.ds(tap, 1), :], (SUB, LANES))


def masked_taps(plan, taps, table):
    for part in plan.sections:
        side, pitch = part["side"], part["pitch"]
        place = lax.broadcasted_iota(jnp.int32, (pitch, LANES), 0)
        for tap in range(side):
            row = taps[pl.ds(part["tap"] + tap, 1), :]
            table[pl.ds(part["mask_row"] + tap * pitch, pitch), :] = jnp.where(place >= tap, row, 0.0)


def forward_kernel(plan, where_far, block, height_far, width_far, skip_far, out_far, packed, across, first, second, image, where, px, pu, height_wide, width_masked, sems, *rest):
    height, width, skip, out, left = rest
    small = started([(height_far, height), (width_far, width), (skip_far, skip)], sems.at[pl.ds(3, 3)])
    masks = slot_masks(plan)
    indices = pltpu.make_async_copy(where_far, where, sems.at[0])
    indices.start()
    px[pl.ds(0, MARGIN), :] = jnp.zeros((MARGIN, LANES), F32)
    for copy in small:
        copy.wait()
    wide_taps(plan, height, height_wide)
    masked_taps(plan, width, width_masked)
    indices.wait()
    scatter_rows(plan, where, block, (first, second), image)
    pack_images(plan, masks, image, px, MARGIN)
    skips = jnp.broadcast_to(skip[...], (SUB, LANES))
    for part in plan.sections:
        side, pitch = part["side"], part["pitch"]
        area = side * pitch

        def group(t, carry, part=part, side=side, pitch=pitch, area=area):
            start = MARGIN + part["packed_row"] + t * area

            for j in range(0, pitch, SUB):
                reach = range(min(side, j + SUB))
                weights = [width_masked[pl.ds(part["mask_row"] + tap * pitch + j, SUB), :] for tap in reach]

                def line(i, inner, j=j, weights=weights):
                    base = start + i * pitch + j
                    total = weights[0] * px[pl.ds(pl.multiple_of(base, SUB), SUB), :]
                    for tap in range(1, len(weights)):
                        total = total + weights[tap] * px[pl.ds(base - tap, SUB), :]
                    pu[pl.ds(pl.multiple_of(base, SUB), SUB), :] = total
                    return inner

                lax.fori_loop(0, side, line, 0, unroll=2)

            def column(c, inner):
                first = pl.multiple_of(start + c * SUB, SUB)
                held = [pu[pl.ds(pl.multiple_of(first + k * pitch, SUB), SUB), :] for k in range(side)]
                for i in range(side):
                    total = skips * px[pl.ds(pl.multiple_of(first + i * pitch, SUB), SUB), :]
                    for k in range(i + 1):
                        total = total + height_wide[pl.ds((part["tap"] + i - k) * SUB, SUB), :] * held[k]
                    unpack_line(plan, masks, part, t, i * pitch + c * SUB, total, image)
                return inner

            lax.fori_loop(0, pitch // SUB, column, 0)
            return carry

        lax.fori_loop(0, part["groups"], group, 0)
    kept = [(px.at[pl.ds(MARGIN, plan.packed_rows)], packed), (pu.at[pl.ds(MARGIN, plan.packed_rows)], across)]
    kept = started(kept, sems.at[pl.ds(1, 2)])
    leaving = lambda s: pltpu.make_async_copy(out.at[s], out_far.at[s], left.at[s])
    gather_rows(plan, where, (first, second), image, out, leave=lambda s: leaving(s).start())
    for copy in kept:
        copy.wait()

    def gone(s, carry):
        leaving(s).wait()
        return carry

    lax.fori_loop(0, plan.devices, gone, 0)


def arrive_kernel(plan, where_far, block_far, act_far, weight_far, given_far, tokens_far, out_grad_far, sums_far, pre_sum_far, *rest):
    grads, block_out, shares, mark, *rest = rest[-20:]
    where, block, first, second, image, act, weight_out, given, tokens, out_grad, sums, pre_sum, branch, rows, came, sems = rest
    mark[...] = jnp.zeros_like(mark)
    soon = started([(block_far, block), (where_far, where)], came.at[pl.ds(2, 2)])
    arriving = started([(act_far, act), (weight_far, weight_out)], came.at[pl.ds(0, 2)])
    there = [(given_far, given), (tokens_far, tokens), (out_grad_far, out_grad), (sums_far, sums), (pre_sum_far, pre_sum)]
    later = started(there, sems)

    def ready():
        for copy in arriving:
            copy.wait()

    def product(k):
        lanes = pl.ds(pl.multiple_of(k * LANES, LANES), LANES)
        branch[:, lanes] = jnp.dot(act[...], weight_out[:, lanes], preferred_element_type=F32)

    for copy in soon:
        copy.wait()
    scatter_rows(plan, where, block, (first, second), image, product, tokens.shape[1] // LANES, ready)
    for copy in later:
        copy.wait()
    scale, bias_out, bias_row = (given[pl.ds(i, 1), :] for i in range(3))
    total = branch[...] + bias_out
    block_out[...] = (tokens[...].astype(F32) + scale * total).astype(BF16)
    scale_row = jnp.sum(out_grad[...].astype(F32) * total, axis=0, keepdims=True)
    shares[...] = small_shares(plan, sums[...], pre_sum[...], bias_row, scale_row, rows)
    pack_images(plan, slot_masks(plan), image, grads, 0)


def leave_kernel(plan, where_far, grads, extra, *rest):
    out, mark, near, far, image, halves, where, sem = rest[-8:]
    indices = pltpu.make_async_copy(where_far, where, sem)
    indices.start()
    mark[...] = jnp.zeros_like(mark)
    masks = slot_masks(plan)
    for part in plan.sections:
        area = part["side"] * part["pitch"]

        def group(t, carry, part=part, area=area):
            for offset in range(0, area, SUB):
                row = pl.multiple_of(part["packed_row"] + t * area + offset, SUB)
                unpack_line(plan, masks, part, t, offset, grads[pl.ds(row, SUB), :], image)
            return carry

        lax.fori_loop(0, part["groups"], group, 0)
    indices.wait()
    exact = extra[...]
    high = exact.astype(BF16).astype(F32)
    lane = lax.broadcasted_iota(jnp.int32, exact.shape, 1)
    halves[...] = jnp.where(lane < plan.extra_lane + SUB, high, exact - high)
    gather_rows(plan, where, (near, far), image, out, halves)


def backward_kernel(plan, pg, height, width, skip, packed_far, across_far, *rest):
    out, height_sums, width_sums, skip_sums, mark, pd, height_wide, width_wide, packed, across, sems = rest[-11:]
    mark[...] = jnp.zeros_like(mark)
    arriving = started([(across_far, across), (packed_far, packed)], sems)
    place = lax.broadcasted_iota(jnp.int32, (SUB, LANES), 0)
    pd[pl.ds(plan.packed_rows, MARGIN), :] = jnp.zeros((MARGIN, LANES), F32)
    wide_taps(plan, height, height_wide)
    wide_taps(plan, width, width_wide)
    skips = jnp.broadcast_to(skip[...], (SUB, LANES))
    skip_sums[...] = jnp.zeros((SUB, LANES), F32)
    height_sums[...] = jnp.zeros((TAPS * SUB, LANES), F32)
    for part in plan.sections:
        side, pitch = part["side"], part["pitch"]
        area = side * pitch

        def group(t, carry, part=part, side=side, pitch=pitch, area=area):
            start = part["packed_row"] + t * area

            def column(c, inner):
                first = pl.multiple_of(start + c * SUB, SUB)
                rows = [pl.ds(pl.multiple_of(first + k * pitch, SUB), SUB) for k in range(side)]
                held = [pg[row, :] for row in rows]
                for k in range(side):
                    total = jnp.zeros((SUB, LANES), F32)
                    for i in range(k, side):
                        total = total + height_wide[pl.ds((part["tap"] + i - k) * SUB, SUB), :] * held[i]
                    pd[rows[k], :] = total
                return inner

            lax.fori_loop(0, pitch // SUB, column, 0)
            return carry

        lax.fori_loop(0, part["groups"], group, 0)
    arriving[0].wait()
    for part in plan.sections:
        side, pitch = part["side"], part["pitch"]
        area = side * pitch

        def group(t, carry, part=part, side=side, pitch=pitch, area=area):
            start = part["packed_row"] + t * area

            def column(c, inner):
                first = pl.multiple_of(start + c * SUB, SUB)
                rows = [pl.ds(pl.multiple_of(first + k * pitch, SUB), SUB) for k in range(side)]
                held = [pg[row, :] for row in rows]
                ways = [across[row, :] for row in rows]
                for tap in range(side):
                    total = held[tap] * ways[0]
                    for k in range(1, side - tap):
                        total = total + held[k + tap] * ways[k]
                    height_sums[pl.ds((part["tap"] + tap) * SUB, SUB), :] += total
                return inner

            lax.fori_loop(0, pitch // SUB, column, 0)
            return carry

        lax.fori_loop(0, part["groups"], group, 0)
    arriving[1].wait()
    for part in plan.sections:
        side, pitch = part["side"], part["pitch"]
        area = side * pitch

        def group(t, carry, part=part, side=side, pitch=pitch, area=area):
            start = part["packed_row"] + t * area

            def line(i, sums):
                sums = list(sums)
                base = start + i * pitch
                aligned = pl.multiple_of(base, SUB)
                for j in range(0, pitch, SUB):
                    here = pl.ds(pl.multiple_of(aligned + j, SUB), SUB)
                    mine, grad = packed[here, :], pg[here, :]
                    total = skips * grad
                    sums[side] = sums[side] + mine * grad
                    for tap in range(min(side, side - j)):
                        moved = pd[pl.ds(base + j + tap, SUB), :]
                        if j + SUB - 1 + tap >= pitch:
                            moved = jnp.where(place + (j + tap) < side, moved, 0.0)
                        total = total + width_wide[pl.ds((part["tap"] + tap) * SUB, SUB), :] * moved
                        sums[tap] = sums[tap] + mine * moved
                    out[here, :] = total
                return tuple(sums)

            return lax.fori_loop(0, side, line, carry)

        zero = jnp.zeros((SUB, LANES), F32)
        sums = lax.fori_loop(0, part["groups"], group, (zero,) * (side + 1))
        for tap in range(side):
            width_sums[pl.ds((part["tap"] + tap) * SUB, SUB), :] = sums[tap]
        skip_sums[...] += sums[side]


def whole(memory):
    return pl.BlockSpec(memory_space=memory)


def lanes_of(rows):
    return jax.ShapeDtypeStruct((rows, LANES), F32)


def row_buffers(plan):
    return [pltpu.VMEM((plan.row_pad, LANES), F32)] * 2 + [pltpu.VMEM((plan.image_rows, LANES), F32)]


def near(values):
    return pltpu.with_memory_space_constraint(values, pltpu.VMEM)


def distant(values):
    return pltpu.with_memory_space_constraint(values, pltpu.HBM)


def kernel_call(kernel, name, micros, memories, out_shape, scratch, args, after=(), stays=(), held=(), left=()):
    single = not isinstance(out_shape, tuple)
    shapes = (out_shape,) if single else out_shape
    shapes = tuple((pltpu.VMEM if i in stays else pltpu.HBM)(o.shape, o.dtype) for i, o in enumerate(shapes))
    outs = tuple(whole(pltpu.VMEM) for _ in shapes)
    place = lambda i, value: near(value) if i in held else value if memories[i] is pltpu.SMEM or i in left else distant(value)
    out = pl.pallas_call(
        kernel,
        out_shape=shapes,
        in_specs=[whole(m) for m in memories] + [whole(pltpu.HBM)] * len(after),
        out_specs=outs,
        scratch_shapes=scratch,
        compiler_params=pltpu.CompilerParams(vmem_limit_bytes=LESS if stays or held else VMEM),
        cost_estimate=pl.CostEstimate(flops=1_000_000, bytes_accessed=int(3_690_000 * micros), transcendentals=0),
        name=name,
    )(*[place(i, value) for i, value in enumerate(args)], *map(distant, after))
    return out[0] if single else out


def mixer_forward(plan, where, block, height, width, skip):
    rows = plan.packed_rows
    ins = [(where, FAR), (block, NEAR), (height, FAR), (width, FAR), (skip, FAR)]
    outs = [(block.shape, BF16, FAR), ((rows, LANES), F32, FAR), ((rows, LANES), F32, FAR)]
    room = row_buffers(plan) + [
        pltpu.SMEM(where.shape, jnp.int32),
        pltpu.VMEM((rows + MARGIN, LANES), F32),
        pltpu.VMEM((rows + MARGIN, LANES), F32),
        pltpu.VMEM((TAPS * SUB, LANES), F32),
        pltpu.VMEM((plan.mask_rows, LANES), F32),
        pltpu.SemaphoreType.DMA((6,)),
        *[pltpu.VMEM(value.shape, F32) for value in (height, width, skip)],
        pltpu.VMEM(block.shape, BF16),
        pltpu.SemaphoreType.DMA((plan.devices,)),
    ]
    return run(functools.partial(forward_kernel, plan), "mixer_forward", ins, outs, room, micros=30, limit=LESS)


def mixer_arrive(plan, where, block, act, weight_out, given, tokens, out_grad, sums, pre_sum, after):
    ins = [(value, FAR) for value in (where, block, act, weight_out, given, tokens, out_grad, sums, pre_sum)]
    width = tokens.shape[1]
    outs = [((plan.packed_rows, LANES), F32, NEAR), (tokens.shape, BF16, AUTO), ((width, LANES), F32, AUTO), ((SUB, LANES), F32, AUTO)]
    room = [pltpu.SMEM(where.shape, jnp.int32), pltpu.VMEM(block.shape, BF16)] + row_buffers(plan) + [pltpu.VMEM(value.shape, value.dtype) for value in (act, weight_out, given, tokens, out_grad, sums, pre_sum)]
    room += [pltpu.VMEM(tokens.shape, F32), pltpu.VMEM((LANES, width), F32), pltpu.SemaphoreType.DMA((4,)), pltpu.SemaphoreType.DMA((5,))]
    return run(functools.partial(arrive_kernel, plan), "mixer_arrive", ins, outs, room, after, limit=LESS)


def mixer_backward(plan, grads, height, width, skip, packed, across, after):
    rows = plan.packed_rows
    ins = [(grads, NEAR), (height, AUTO), (width, AUTO), (skip, AUTO), (packed, FAR), (across, FAR)]
    outs = [((rows, LANES), F32, NEAR)] + [((size, LANES), F32, AUTO) for size in (TAPS * SUB, TAPS * SUB, SUB, SUB)]
    room = [pltpu.VMEM((size, LANES), F32) for size in (rows + MARGIN, TAPS * SUB, TAPS * SUB, rows, rows)]
    room += [pltpu.SemaphoreType.DMA((2,))]
    return run(functools.partial(backward_kernel, plan), "mixer_backward", ins, outs, room, after, limit=LESS)


def mixer_leave(plan, where, grads, extra, after):
    ins = [(where, FAR), (grads, NEAR), (extra, AUTO)]
    outs = [((plan.devices, plan.channels, plan.row_pad), BF16, AUTO), ((SUB, LANES), F32, AUTO)]
    room = row_buffers(plan) + [pltpu.VMEM(extra.shape, F32), pltpu.SMEM(where.shape, jnp.int32), pltpu.SemaphoreType.DMA]
    return run(functools.partial(leave_kernel, plan), "mixer_leave", ins, outs, room, after, limit=LESS)


def taps_kernel(plan, coef_height, rate_height, coef_width, rate_width, spread, height_sums, width_sums, skip_sums, *rest):
    outs = rest[-5:]
    reach, scale = tap_places()
    fold = lambda sums: lax.dot_general(spread[...], sums, (((1,), (1,)), ((), ())), precision=lax.Precision.HIGHEST, preferred_element_type=F32)
    for coef, log_rate, sums, coef_out, rate_out in (
        (coef_height, rate_height, height_sums, outs[0], outs[1]),
        (coef_width, rate_width, width_sums, outs[2], outs[3]),
    ):
        grads = fold(sums[...].reshape(TAPS, SUB, LANES).sum(axis=1))
        rate = jnp.exp(log_rate[...])
        plain, moved = jnp.zeros_like(rate), jnp.zeros_like(rate)
        for tap in range(TAPS):
            weighted = (grads[:, tap : tap + 1] * float(scale[tap])) * jnp.exp(rate * float(-reach[tap]))
            plain = plain + weighted
            moved = moved + weighted * float(reach[tap])
        coef_out[...] = plain
        rate_out[...] = -coef[...] * rate * moved
    total = jnp.sum(skip_sums[...], axis=0, keepdims=True)
    outs[4][...] = lax.dot_general(total, spread[...], (((1,), (1,)), ((), ())), precision=lax.Precision.HIGHEST, preferred_element_type=F32)


def tap_grads(plan, coefs, spread, sums, after):
    shape = jax.ShapeDtypeStruct(coefs[0].shape, F32)
    outs = (shape,) * 4 + (jax.ShapeDtypeStruct((1, plan.channels), F32),)
    *grads, skips = kernel_call(functools.partial(taps_kernel, plan), "tap_grads", 0.01, [pltpu.VMEM] * 8, outs, [], (*coefs, spread, *sums), after)
    return *grads, skips[0]


def tokens_kernel(plan, blocks, out_grad, out, *rest):
    smalls, flipped = rest[:-1], rest[-1]
    total = jnp.zeros((plan.channels, LANES), F32)
    for s in range(plan.devices):
        block = blocks[s].astype(F32)
        flipped[pl.ds(s * plan.channels, plan.channels), :] = block[:, : plan.rows]
        total = total + block[:, plan.row_pad - LANES :]
    first = plan.extra_lane
    rows = total.T
    rows = rows[first : first + SUB] + rows[first + SUB : first + 2 * SUB]
    kind = 0
    for small in smalls:
        for i in range(small.shape[1] // plan.channels):
            small[:, pl.ds(i * plan.channels, plan.channels)] = rows[kind : kind + 1]
            kind += 1
    out[...] = out_grad[...].astype(F32) + flipped[...].T


def token_grads(plan, blocks, out_grad, kinds):
    outs = [(out_grad.shape, F32, AUTO)] + [((1, count * plan.channels), F32, AUTO) for count in (1, 1, kinds, 1, 1)]
    room = [pltpu.VMEM(out_grad.shape[::-1], F32)]
    return run(functools.partial(tokens_kernel, plan), "token_grads", [(blocks, NEAR), (out_grad, AUTO)], outs, room)


def started(pairs, sems):
    copies = [pltpu.make_async_copy(source, target, sems.at[i]) for i, (source, target) in enumerate(pairs)]
    for copy in copies:
        copy.start()
    return copies


NEAR, FAR, AUTO, OPEN, SCALAR = "near", "far", "auto", "open", "scalar"


def run(kernel, name, ins, outs, scratch, after=(), micros=0.01, limit=VMEM):
    same = lambda value: value
    memory = {NEAR: pltpu.VMEM, FAR: pltpu.HBM, AUTO: pltpu.VMEM, OPEN: pltpu.VMEM, SCALAR: pltpu.SMEM}
    hold = {NEAR: near, FAR: distant, AUTO: distant, OPEN: same, SCALAR: same}
    make = {NEAR: pltpu.VMEM, FAR: pltpu.HBM, AUTO: pltpu.HBM, OPEN: jax.ShapeDtypeStruct}
    return pl.pallas_call(
        kernel,
        out_shape=tuple(make[place](shape, dtype) for shape, dtype, place in outs),
        in_specs=[whole(memory[place]) for _, place in ins] + [whole(pltpu.HBM)] * len(after),
        out_specs=tuple(whole(memory[place]) for _, _, place in outs),
        scratch_shapes=scratch,
        compiler_params=pltpu.CompilerParams(vmem_limit_bytes=limit),
        cost_estimate=pl.CostEstimate(flops=1000, bytes_accessed=int(3_690_000 * micros), transcendentals=0),
        name=name,
    )(*[hold[place](value) for value, place in ins], *map(distant, after))


def feed_kernel(plan, blocks, gain_far, bias_far, weight_far, bias_in_far, grad_act_far, grads_far, act_far, sums_far, pre_sum_far, keep_far, *rest):
    sent, scratch = rest[:-18], rest[-18:]
    normed, flipped, unit, total, weight_in, grad_act, act, grad_pre, keep, other, came, left = scratch[:12]
    gain, bias, bias_in, grads, sums, pre_sum = scratch[12:]
    channels, count = plan.channels, plan.devices
    width, hidden = weight_in.shape
    chunks, chips, _, _ = keep.shape
    tile, each = hidden // chunks, len(sent) // chunks
    core = own_bit(0)
    parts = [pl.ds(i * tile, tile) for i in range(chunks)]
    small = started([(gain_far, gain), (bias_far, bias), (bias_in_far, bias_in)], came.at[pl.ds(2 * chunks, 3)])
    arriving = []
    for i, at in enumerate(parts):
        there = [(weight_far.at[:, at], weight_in.at[:, at]), (grad_act_far.at[:, at], grad_act.at[:, at])]
        arriving.append(started(there, came.at[pl.ds(2 * i, 2)]))
    for s in range(count):
        unit[pl.ds(s * channels, channels), :] = blocks[s].astype(F32)
    mean = jnp.sum(unit[...], axis=0, keepdims=True) * (1.0 / width)
    centred = unit[...] - mean
    inverse = lax.rsqrt(jnp.sum(centred * centred, axis=0, keepdims=True) * (1.0 / width) + EPSILON)
    unit[...] = centred * inverse
    for copy in small:
        copy.wait()
    scaled = unit[...] * gain[...] + bias[...]
    flipped[...] = scaled.astype(BF16)
    normed[...] = scaled.T.astype(BF16)
    leaving = []

    def activate(i):
        at = parts[i]
        for copy in (arriving[0] if i == 0 else arriving[1] + arriving[2] if i == 1 else []):
            copy.wait()
        pre = jnp.dot(normed[...], weight_in[:, at], preferred_element_type=F32) + bias_in[:, at]
        cdf = 0.5 * (1.0 + lax.erf(pre * math.sqrt(0.5)))
        act[:, at] = (pre * cdf).astype(BF16)
        slope = cdf + pre * jnp.exp(-0.5 * pre * pre) * (1.0 / math.sqrt(2.0 * math.pi))
        grad = grad_act[:, at] * slope
        pre_sum[:, at] = jnp.sum(grad, axis=0, keepdims=True)
        grad_pre[:, at] = grad.astype(BF16)

    def leave(there):
        leaving.extend(started(there, left.at[pl.ds(len(leaving), len(there))]))

    activate(0)
    for i, at in enumerate(parts):
        if i + 1 < chunks:
            activate(i + 1)
        leave([(act.at[:, at], act_far.at[:, at])])
        part = jnp.dot(flipped[...], grad_pre[:, at], preferred_element_type=F32)
        for c in range(chips):
            first = part[2 * c * channels : (2 * c + 1) * channels]
            second = part[(2 * c + 1) * channels : (2 * c + 2) * channels]
            keep[i, c] = retiled(jnp.where(core == 0, first, second), width).astype(BF16)
            other[i, c] = retiled(jnp.where(core == 0, second, first), width).astype(BF16)
        there = [(other.at[i, :, :, lanes], sent[i * each + p]) for p, lanes in enumerate(lane_parts(width, each))]
        leave(there + [(keep.at[i], keep_far.at[i])])
        back = lax.dot_general(grad_pre[:, at], weight_in[:, at], (((1,), (1,)), ((), ())), preferred_element_type=F32)
        total[...] = back if i == 0 else total[...] + back
    turned = total[...].T
    grad = turned * gain[...]
    level = jnp.sum(grad, axis=0, keepdims=True) * (1.0 / width)
    tilt = jnp.sum(grad * unit[...], axis=0, keepdims=True) * (1.0 / width)
    total_low = (inverse * (grad - level - unit[...] * tilt)).astype(BF16)
    for s in range(count):
        grads[s] = total_low[s * channels : (s + 1) * channels]
    leave([(grads, grads_far)])
    lane = lax.broadcasted_iota(jnp.int32, sums.shape, 1)
    sums[...] = jnp.where(
        plan.kind(lane, 0),
        jnp.sum(turned * unit[...], axis=1, keepdims=True),
        jnp.where(plan.kind(lane, 1), jnp.sum(turned, axis=1, keepdims=True), 0.0),
    )
    leave([(sums, sums_far), (pre_sum, pre_sum_far)])
    for copy in leaving:
        copy.wait()


def feed(plan, blocks, gain, bias, weight_in, bias_in, grad_act):
    rows, width, hidden, chips = plan.rows, plan.devices * plan.channels, weight_in.shape[1], plan.devices // 2
    high, each = plan.channels * hidden // CHUNKS // width, 2
    ins = [(blocks, NEAR)] + [(value, FAR) for value in (gain[:, None], bias[:, None], weight_in, bias_in[None], grad_act)]
    outs = [
        (blocks.shape, BF16, FAR),
        ((rows, hidden), BF16, FAR),
        ((width, LANES), F32, FAR),
        ((1, hidden), F32, FAR),
        ((CHUNKS, chips, high, width), BF16, FAR),
    ] + [((chips, high, width // each), BF16, FAR)] * (CHUNKS * each)
    room = [
        pltpu.VMEM((rows, width), BF16),
        pltpu.VMEM((width, rows), BF16),
        pltpu.VMEM((width, rows), F32),
        pltpu.VMEM((rows, width), F32),
        pltpu.VMEM((width, hidden), BF16),
        pltpu.VMEM((rows, hidden), F32),
        pltpu.VMEM((rows, hidden), BF16),
        pltpu.VMEM((rows, hidden), BF16),
        pltpu.VMEM((CHUNKS, chips, high, width), BF16),
        pltpu.VMEM((CHUNKS, chips, high, width), BF16),
        pltpu.SemaphoreType.DMA((2 * CHUNKS + 3,)),
        pltpu.SemaphoreType.DMA((CHUNKS * (each + 2) + 3,)),
        pltpu.VMEM((width, 1), F32),
        pltpu.VMEM((width, 1), F32),
        pltpu.VMEM((1, hidden), F32),
        pltpu.VMEM(blocks.shape, BF16),
        pltpu.VMEM((width, LANES), F32),
        pltpu.VMEM((1, hidden), F32),
    ]
    grads, act, sums, pre_sum, keep, *sent = run(functools.partial(feed_kernel, plan), "feed_forward", ins, outs, room, micros=10, limit=LESS)
    return grads, act, sums, pre_sum, keep, sent


def out_grad_kernel(act_far, scaled_far, keep_far, *rest):
    sent, (act, scaled, keep, other, came, left) = rest[:-6], rest[-6:]
    core = own_bit(0)
    chunks, chips, high, width = keep.shape
    height, steps = chunks * high, came.shape[0] - 1
    tile, each, part = act.shape[1] // steps, chips // steps, chips // len(sent)
    parts = [pl.ds(i * tile, tile) for i in range(steps)]
    arriving, leaving = started([(scaled_far, scaled)] + [(act_far.at[:, at], act.at[:, at]) for at in parts], came), []
    arriving[0].wait()
    for i, at in enumerate(parts):
        arriving[1 + i].wait()
        low = lax.dot_general(act[:, at], scaled[...], (((0,), (0,)), ((), ())), preferred_element_type=F32).astype(BF16)
        for c in range(each):
            first = low[2 * c * height : (2 * c + 1) * height]
            second = low[(2 * c + 1) * height : (2 * c + 2) * height]
            mine, yours = jnp.where(core == 0, first, second), jnp.where(core == 0, second, first)
            for chunk in range(chunks):
                keep[chunk, i * each + c] = mine[chunk * high : (chunk + 1) * high]
                other[chunk, i * each + c] = yours[chunk * high : (chunk + 1) * high]
        some = pl.ds(i * each, each)
        there = [(other.at[:, pl.ds(p * part, part)], sent[p]) for p in range(i * each // part, (i + 1) * each // part)]
        there += [(keep.at[:, some], keep_far.at[:, some])]
        leaving += started(there, left.at[pl.ds(len(leaving), len(there))])
    for copy in leaving:
        copy.wait()


def out_grad_halves(plan, act, scaled):
    hidden, width, chips = act.shape[1], scaled.shape[1], plan.devices // 2
    high, steps, pieces = hidden // plan.devices // CHUNKS, hidden // 768, 4
    ins = [(act, FAR), (scaled, FAR)]
    outs = [((CHUNKS, chips, high, width), BF16, FAR)] + [((CHUNKS, chips // pieces, high, width), BF16, FAR)] * pieces
    room = [pltpu.VMEM(value.shape, BF16) for value in (act, scaled)] + [pltpu.VMEM(outs[0][0], BF16)] * 2
    room += [pltpu.SemaphoreType.DMA((1 + steps,)), pltpu.SemaphoreType.DMA((pieces + steps,))]
    keep, *sent = run(out_grad_kernel, "out_grad_halves", ins, outs, room)
    return keep, sent


def own_bit(bit):
    return lax.axis_index("chan") >> bit & 1


def lane_parts(width, count):
    return [pl.ds(p * (width // count), width // count) for p in range(count)]


def retiled(values, width):
    tiles = [values[r : r + SUB, c : c + LANES] for r in range(0, values.shape[0], SUB) for c in range(0, values.shape[1], LANES)]
    each = width // LANES
    return jnp.concatenate([jnp.concatenate(tiles[i : i + each], axis=1) for i in range(0, len(tiles), each)], axis=0)


def small_shares(plan, sums, pre_sum, bias_row, scale_row, rows):
    channels, count = plan.channels, plan.devices
    width = channels * count
    kinds = pre_sum.shape[1] // width
    lane = lax.broadcasted_iota(jnp.int32, sums.shape, 1)
    rows[...] = jnp.zeros_like(rows)
    for kind, row in ((2 + kinds, bias_row), (3 + kinds, scale_row)):
        for again in (0, SUB):
            rows[pl.ds(plan.extra_lane + kind + again, 1), :] = row
    total = sums + rows[...].T
    columns = jnp.broadcast_to(pre_sum, (SUB, pre_sum.shape[1])).T.reshape(count, kinds, channels, SUB)
    for kind in range(kinds):
        column = columns[:, kind].reshape(width, SUB)[:, :1]
        total = total + jnp.where(plan.kind(lane, 2 + kind), column, 0.0)
    return total


def held_back(arrays, after):
    kept = len(arrays)
    return pl.pallas_call(
        lambda *refs: None,
        out_shape=tuple(pltpu.HBM(a.shape, a.dtype) for a in arrays),
        in_specs=[whole(pltpu.HBM)] * kept + [whole(pl.ANY)] * len(after),
        out_specs=(whole(pltpu.HBM),) * kept,
        input_output_aliases={i: i for i in range(kept)},
        cost_estimate=pl.CostEstimate(flops=0, bytes_accessed=0, transcendentals=0),
        name="held_back",
    )(*map(distant, arrays), *after)


def act_grads_kernel(scaled, weight_out, *rest):
    out = rest[-1]
    tile = 768
    for c in range(0, out.shape[1], tile):
        part = lax.dot_general(scaled[...], weight_out[pl.ds(c, tile), :], (((1,), (1,)), ((), ())), preferred_element_type=F32)
        out[:, pl.ds(c, tile)] = part


def act_grads(scaled, weight_out, after):
    outs = [((scaled.shape[0], weight_out.shape[0]), F32, AUTO)]
    return run(act_grads_kernel, "act_grads", [(scaled, AUTO), (weight_out, AUTO)], outs, [], after, micros=6)[0]


def merge_entries(at, bit, keep, got, mine, other):
    low = (1 << at) - 1
    for e in range(mine.shape[0]):
        first = (e >> at << at + 1) + (e & low)
        here, there = first + bit * (low + 1), first + (1 - bit) * (low + 1)
        other[e] = keep(there) + got(there, first)
        mine[e] = keep(here) + got(here, first)


def first_merge_kernel(cuts, counts, *refs):
    outs, mark, scratch = refs[-12:-6], refs[-6], refs[-5:]
    mark[...] = jnp.zeros_like(mark)
    sems, groups, used, at, places = scratch[-1], [], 0, 0, []
    for which, count in enumerate(counts):
        keep, came, got = scratch[2 * which], scratch[2 * which + 1], refs[at + 1 : at + 1 + count]
        places.append(got)
        chunks, chips, high, width = keep.shape
        for i in range(chunks):
            there = [(refs[at].at[i], keep.at[i])]
            if len(got[0].shape) == 4:
                part = chips // count
                if i == chunks - 1:
                    there += [(piece.at[i], came.at[i, pl.ds(p * part, part)]) for p, piece in enumerate(got)]
            else:
                each = count // chunks
                there += [(got[i * each + p], came.at[i, :, :, lanes]) for p, lanes in enumerate(lane_parts(width, each))]
            groups.append(started(there, sems.at[pl.ds(used, len(there))]))
            used += len(there)
        at += 1 + count
    for which in range(2):
        keep, came = scratch[2 * which], scratch[2 * which + 1]
        chunks, _, high, _ = keep.shape
        for i in range(chunks):
            for copy in groups[which * chunks + i]:
                copy.wait()
            pair, row = (which, i * high) if i < chunks - 1 else (2, which * high)
            cut, bit = cuts[pair]
            mine, other = (out.at[:, pl.ds(row, high)] for out in outs[2 * pair : 2 * pair + 2])
            new = lambda e, first: came[i, e]
            if len(places[which][0].shape) == 4 and i < chunks - 1:
                part = places[which][0].shape[1]
                new = lambda e, first: places[which][first // part][i, e - first // part * part]
            merge_entries(cut, own_bit(bit), lambda e: keep[i, e], new, mine, other)


def first_merge(parts, cuts, after):
    chunks, chips, high, width = parts[0][0].shape
    ins = [(value, place) for (keep, got), near_by in zip(parts, (FAR, NEAR)) for value, place in ((keep, FAR), *((piece, near_by) for piece in got))]
    outs = [((chips // 2, rows, width), BF16, NEAR) for rows in ((chunks - 1) * high, (chunks - 1) * high, 2 * high) for _ in range(2)]
    room = [pltpu.VMEM(keep.shape, BF16) for keep, _ in parts for _ in range(2)] + [pltpu.SemaphoreType.DMA((64,))]
    kernel = functools.partial(first_merge_kernel, cuts, [len(got) for _, got in parts])
    *halves, mark = run(kernel, "first_merge", ins, outs + [((SUB, LANES), F32, AUTO)], room, after, limit=LESS)
    return halves[0::2], halves[1::2], mark


def merge_kernel(jobs, *refs):
    count, pairs = sum(len(job) for job in jobs), 2 * len(jobs)
    outs, mark = refs[-1 - pairs : -1], refs[-1]
    mark[...] = jnp.zeros_like(mark)
    i = 0
    for j, job in enumerate(jobs):
        row = 0
        for at, bit in job:
            keep, got = refs[i], refs[count + i]
            rows = pl.ds(row, keep.shape[1])
            merge_entries(at, own_bit(bit), lambda e: keep[e], lambda e, first: got[e], outs[2 * j].at[:, rows], outs[2 * j + 1].at[:, rows])
            row += keep.shape[1]
            i += 1


def merge(keeps, gots, jobs, after=()):
    ins = [(value, NEAR) for value in keeps] + [(value, OPEN) for value in gots]
    outs, i = [], 0
    for job in jobs:
        parts = keeps[i : i + len(job)]
        i += len(job)
        outs += [((parts[0].shape[0] // 2, sum(part.shape[1] for part in parts), parts[0].shape[2]), BF16, NEAR)] * 2
    *halves, mark = run(functools.partial(merge_kernel, jobs), "merge_halves", ins, outs + [((SUB, LANES), F32, AUTO)], [], after, limit=LESS)
    return halves[0::2], halves[1::2], mark


def last_kernel(keep, got, less_keep, less_got, in_sum, out_sum):
    total = keep[0].astype(F32) + got[0].astype(F32)
    less = less_keep[0].astype(F32) + less_got[0].astype(F32)
    high = less.shape[0] // 2
    tile = in_sum.shape[1] // CHUNKS
    for i, part in enumerate((total[:high], total[high : 2 * high], less[:high])):
        in_sum[:, pl.ds(i * tile, tile)] = retiled(part, tile)
    out_sum[pl.ds(0, 2 * high), :] = total[2 * high :]
    out_sum[pl.ds(2 * high, high), :] = less[high:]


def last_sums(parts, channels, hidden, after):
    ins = [(parts[0], NEAR), (parts[1], OPEN), (parts[2], NEAR), (parts[3], OPEN)]
    high, width = parts[2].shape[1] // 2, parts[2].shape[2]
    outs = [((channels, hidden), F32, AUTO), ((CHUNKS * high, width), F32, AUTO)]

    def kernel(*refs):
        last_kernel(*refs[:4], *refs[-2:])

    return run(kernel, "last_sums", ins, outs, [], after)


def tap_places():
    reach = np.concatenate([np.arange(s) / s for s in SIDES]).astype(np.float32)
    scale = np.concatenate([np.full(s, 1.0 / math.sqrt(s)) for s in SIDES]).astype(np.float32)
    return reach, scale


def profiles(coefficient, log_rate):
    reach, scale = tap_places()
    decayed = jnp.exp(-jnp.exp(log_rate)[None] * reach[:, None, None])
    return jnp.sum(coefficient[None] * decayed, axis=2) * scale[:, None]


def profile_grads(coefficient, log_rate, grads):
    reach, scale = tap_places()
    rate = jnp.exp(log_rate)
    decayed = jnp.exp(-rate[None] * reach[:, None, None])
    weighted = (grads * scale[:, None])[:, :, None] * decayed
    return jnp.sum(weighted, axis=0), -coefficient * rate * jnp.sum(weighted * reach[:, None, None], axis=0)


def kernel_matrix(profile, part):
    side = part["side"]
    offsets = np.arange(side)[:, None] - np.arange(side)[None, :]
    picked = profile[part["tap"] + np.maximum(offsets, 0)]
    return jnp.where((offsets >= 0)[:, :, None], picked, 0.0)


def mix_plain(plan, row_pixel, channel_rows, height, width, skip):
    def one_channel(given):
        values, high, wide, weight = given
        image_order = jnp.zeros_like(values).at[row_pixel].set(values)
        pieces = []
        for part in plan.sections:
            side, count = part["side"], part["images"] * part["side"] ** 2
            block = image_order[part["pixel"] : part["pixel"] + count].reshape(-1, side, side)
            left = kernel_matrix(high[:, None], part)[:, :, 0]
            right = kernel_matrix(wide[:, None], part)[:, :, 0]
            mixed = jnp.einsum("ik,nkl,jl->nij", left, block, right, precision=lax.Precision.HIGHEST)
            pieces.append(mixed.reshape(-1))
        joined = jnp.concatenate(pieces) + weight * image_order
        return joined[row_pixel]

    return lax.map(jax.checkpoint(one_channel), (channel_rows, height.T, width.T, skip))


def exchange(blocks):
    return lax.all_to_all(blocks, "chan", 0, 0, tiled=True)


def to_blocks(rows, devices):
    return rows.T.reshape(devices, rows.shape[1] // devices, rows.shape[0])


def to_rows(blocks):
    return blocks.reshape(-1, blocks.shape[2]).T


def halve(blocks, bits):
    myself = lax.axis_index("chan")
    size = lax.axis_size("chan")
    pairs = lambda bit: [(i, i ^ 1 << bit) for i in range(size)]
    left = list(range(size.bit_length() - 1))
    for bit in bits:
        at = left.index(bit)
        viewed = blocks.reshape((-1, 2, 1 << at) + blocks.shape[1:])
        own = myself >> bit & 1
        keep = lax.dynamic_index_in_dim(viewed, own, 1, keepdims=False)
        send = lax.dynamic_index_in_dim(viewed, 1 - own, 1, keepdims=False)
        got = lax.ppermute(send, "chan", pairs(bit))
        total = keep.astype(F32) + got.astype(F32)
        left.remove(bit)
        blocks = (total if not left else total.astype(BF16)).reshape((-1,) + blocks.shape[1:])
    return blocks[0]


def swapped(x, bit):
    return lax.ppermute(x, "chan", [(i, i ^ 1 << bit) for i in range(lax.axis_size("chan"))])


def body_fast(
    tokens,
    row_pixel,
    coef_height,
    rate_height,
    coef_width,
    rate_width,
    skip_weight,
    norm_gain,
    norm_bias,
    weight_in,
    bias_in,
    weight_out,
    bias_out,
    layer_scale,
    out_grad,
):
    devices = lax.axis_size("chan")
    rows, width_all = tokens.shape
    plan = Plan(devices, rows, width_all // devices)
    token_blocks = exchange(to_blocks(tokens, devices))
    where = plan.address(row_pixel)
    spread = plan.spread()
    taps = (plan.tile_taps(profiles(coef_height, rate_height)), plan.tile_taps(profiles(coef_width, rate_width)), plan.tile_taps(skip_weight[None]))
    mixed_blocks, packed, across = mixer_forward(plan, where, token_blocks, *taps)

    scaled = out_grad.astype(F32) * layer_scale
    scaled_low = scaled.astype(BF16)
    rows_given = jnp.stack([layer_scale, bias_out, jnp.sum(scaled, axis=0)])
    grad_act = act_grads(scaled_low, weight_out, (rows_given,))
    grad_normin, act, sums, pre_sum, in_keep, in_sent = feed(plan, exchange(mixed_blocks), norm_gain, norm_bias, weight_in, bias_in, grad_act)
    grad_blocks = exchange(grad_normin)
    out_keep, out_sent = out_grad_halves(plan, act, scaled_low)
    out_got = [swapped(piece, 0) for piece in out_sent]
    in_got = [swapped(piece, 0) for piece in in_sent]

    x, y, near_z, far_z = range(1, 5)
    swap = lambda parts, bits: [swapped(part, bit) for part, bit in zip(parts, bits)]
    keeps, sends, mark = first_merge(((in_keep, in_got), (out_keep, out_got)), ((0, x), (1, y), (2, near_z)), (grad_blocks,))
    gots = swap(sends, (x, y, near_z))
    grads, block_out, shares, mark = mixer_arrive(plan, where, grad_blocks, act, weight_out, rows_given, tokens, out_grad, sums, pre_sum, (mark,))
    keeps, sends, mark = merge(keeps, gots, (((0, y),), ((0, x),), ((2, far_z),)), (mark,))
    gots = swap(sends, (y, x, far_z))
    grads, *tap_sums, mark = mixer_backward(plan, grads, *taps, packed, across, (mark,))
    both_keeps, both_sends, mark = merge(keeps[:2], gots[:2], (((0, near_z), (0, near_z)),), (mark,))
    both_gots = swap(both_sends, (near_z,))
    leaving, left = mixer_leave(plan, where, grads, shares, (mark,))
    keeps, sends, mark = merge((both_keeps[0], keeps[2]), (both_gots[0], gots[2]), (((0, far_z),), ((0, x),)), (left,))
    (moved,) = held_back((leaving,), (mark,))
    grad_tokens, *smalls = token_grads(plan, exchange(moved), out_grad, pre_sum.shape[1] // width_all)
    both_got, less_got = swap(sends, (far_z, x))
    less_keeps, less_sends, mark = merge(keeps[1:], (less_got,), (((0, y),),))
    (less_got,) = swap(less_sends, (y,))
    coef_grads = tap_grads(plan, (coef_height, rate_height, coef_width, rate_width), spread.astype(F32), tap_sums, (mark,))
    in_sum, out_sum = last_sums(
        (keeps[0], both_got, less_keeps[0], less_got), plan.channels, weight_in.shape[1], (grad_tokens, *coef_grads)
    )
    gain_grad, norm_bias_grad, bias_in_grad, bias_out_grad, scale_grad = (small[0] for small in smalls)
    return (block_out, grad_tokens, *coef_grads, gain_grad, norm_bias_grad, in_sum, bias_in_grad, out_sum, bias_out_grad, scale_grad)


def body_plain(
    tokens,
    row_pixel,
    coef_height,
    rate_height,
    coef_width,
    rate_width,
    skip_weight,
    norm_gain,
    norm_bias,
    weight_in,
    bias_in,
    weight_out,
    bias_out,
    layer_scale,
    out_grad,
):
    devices = lax.axis_size("chan")
    rows, width_all = tokens.shape
    plan = Plan(devices, rows, width_all // devices)
    token_blocks = exchange(to_blocks(tokens, devices))

    height = profiles(coef_height, rate_height)
    width = profiles(coef_width, rate_width)
    lines = lambda blocks: blocks.transpose(1, 0, 2).reshape(blocks.shape[1], -1)
    blocks_of = lambda values: values.astype(BF16).reshape(-1, devices, rows).transpose(1, 0, 2)
    mixed, mixer_back = jax.vjp(
        functools.partial(mix_plain, plan, row_pixel), lines(token_blocks).astype(F32), height, width, skip_weight
    )
    mixed_blocks = blocks_of(mixed)
    normin = to_rows(exchange(mixed_blocks)).astype(F32)

    upstream = out_grad.astype(F32)
    scaled = upstream * layer_scale
    scaled_low = scaled.astype(BF16)
    grad_act = lax.dot_general(scaled_low, weight_out, (((1,), (1,)), ((), ())), preferred_element_type=F32)

    row_mean = jnp.mean(normin, axis=1, keepdims=True)
    centred = normin - row_mean
    inv_std = lax.rsqrt(jnp.mean(centred * centred, axis=1, keepdims=True) + EPSILON)
    unit_rows = centred * inv_std
    normed = (unit_rows * norm_gain + norm_bias).astype(BF16)
    hidden_pre = jnp.dot(normed, weight_in, preferred_element_type=F32) + bias_in
    cdf = 0.5 * (1.0 + lax.erf(hidden_pre * math.sqrt(0.5)))
    act_low = (hidden_pre * cdf).astype(BF16)
    slope = cdf + hidden_pre * jnp.exp(-0.5 * hidden_pre * hidden_pre) * (1.0 / math.sqrt(2.0 * math.pi))
    grad_pre = grad_act * slope
    grad_pre_low = grad_pre.astype(BF16)
    grad_normed = lax.dot_general(grad_pre_low, weight_in, (((1,), (1,)), ((), ())), preferred_element_type=F32)
    grad_unit = grad_normed * norm_gain
    grad_normin = inv_std * (
        grad_unit
        - jnp.mean(grad_unit, axis=1, keepdims=True)
        - unit_rows * jnp.mean(grad_unit * unit_rows, axis=1, keepdims=True)
    )
    grad_blocks = exchange(to_blocks(grad_normin.astype(BF16), devices))

    branch = jnp.dot(act_low, weight_out, preferred_element_type=F32) + bias_out
    block_out = (tokens.astype(F32) + layer_scale * branch).astype(BF16)
    small = (
        jnp.sum(grad_normed * unit_rows, axis=0),
        jnp.sum(grad_normed, axis=0),
        jnp.sum(grad_pre, axis=0),
        jnp.sum(scaled, axis=0),
        jnp.sum(upstream * branch, axis=0),
    )
    weight_in_part = lax.dot_general(normed, grad_pre_low, (((0,), (0,)), ((), ())), preferred_element_type=F32)
    weight_out_part = lax.dot_general(act_low, scaled_low, (((0,), (0,)), ((), ())), preferred_element_type=F32)

    grad_mixed, grad_height, grad_width, grad_skip = mixer_back(lines(grad_blocks).astype(F32))
    grad_rows = blocks_of(grad_mixed)
    coef_height_grad, rate_height_grad = profile_grads(coef_height, rate_height, grad_height)
    coef_width_grad, rate_width_grad = profile_grads(coef_width, rate_width, grad_width)
    grad_tokens = upstream + to_rows(exchange(grad_rows)).astype(F32)

    levels = list(range(devices.bit_length() - 1))
    other = levels[:1] + levels[1:3][::-1] + levels[3:]
    in_sum = halve(weight_in_part.astype(BF16).reshape(devices, -1, weight_in.shape[1]), levels)
    out_sum = halve(weight_out_part.astype(BF16).reshape(devices, -1, weight_out.shape[1]), other)
    shares = jnp.concatenate([s.reshape(devices, -1) for s in small], axis=1)
    shares = exchange(shares).sum(axis=0)
    cuts = np.cumsum([s.shape[0] // devices for s in small])[:-1]
    gain_grad, norm_bias_grad, bias_in_grad, bias_out_grad, scale_grad = jnp.split(shares, cuts)
    return (
        block_out,
        grad_tokens,
        coef_height_grad,
        rate_height_grad,
        coef_width_grad,
        rate_width_grad,
        grad_skip,
        gain_grad,
        norm_bias_grad,
        in_sum,
        bias_in_grad,
        out_sum,
        bias_out_grad,
        scale_grad,
    )


def solution(mesh):
    split, copied = P("chan"), P()

    def body(tokens, *rest):
        devices = lax.axis_size("chan")
        fast = Plan(devices, tokens.shape[0], tokens.shape[1] // devices).fits() and devices == 32
        return (body_fast if fast else body_plain)(tokens, *rest)

    in_specs = (split, copied) + (split,) * 5 + (copied,) * 7 + (split,)
    return jax.shard_map(body, mesh=mesh, in_specs=in_specs, out_specs=(split,) * 14, check_vma=False)
```

profile of v0, /device:TPU:0, one launch (start us, length us, event | category | flops | bytes accessed | tf_op | source)
XLA Modules:
  0.0 195.6 jit_solution(10551728125594809160)
XLA Ops:
  0.7 2.1 %copy.48 = bf16[768,354]{1,0:T(8,128)(2,1)} copy(bf16[768,354]{0,1:T(8,128)(2,1)} %bitcast.11) | data formatting | bytes 1087488 | tf_op jit(solution)/shard_map/transpose | solution.py:936
  2.9 7.3 %all-to-all-start = ((bf16[32,24,354]{2,1,0:T(8,128)(2,1)}), bf16[32,24,354]{2,1,0:T(8,128)(2,1)S(1)}, u32[]{:S(2)}, u32[]{:S(2)}) async-start(bf16[32,24,354]{2,1,0:T(8,128)(2,1)} %bitcast.1), calls=%async_computation | async-start | bytes 1179648 | tf_op jit(solution)/shard_map/all_to_all | solution.py:932
  13.6 13.3 %all-to-all-done.block = bf16[32,24,354]{2,1,0:T(8,128)(2,1)S(1)} async-done(((bf16[32,24,354]{2,1,0:T(8,128)(2,1)}), bf16[32,24,354]{2,1,0:T(8,128)(2,1)S(1)}, u32[]{:S(2)}, u32[]{:S(2)}) %all-to-all-start) | async-done | bytes 543776 | tf_op jit(solution)/shard_map/all_to_all | solution.py:932
  26.9 30.2 %mixer_forward.1 = (bf16[32,24,354]{2,1,0:T(8,128)(2,1)}, f32[3312,128]{1,0:T(8,128)}, f32[3312,128]{1,0:T(8,128)}) custom-call(s32[11328]{0:T(1024)} %select_select_fusion.where_far, bf16[32,24,354]{2,1,0:T(8,128)(2,1)S(1)} %all-to-all-done.block, f32[42,128]{1,0:T(8,128)} %pad.11.height_far.height, f32[42,128]{1,0:T(8,128)} %pad.12.width_far.width, ...), custom_call_target="tpu_custom_call" | custom-call | flops 1000 | bytes 110700000 | tf_op jit(solution)/shard_map/mixer_forward/pallas_call | solution.py:564
  57.1 3.5 %all-to-all-start.1 = ((bf16[32,24,354]{2,1,0:T(8,128)(2,1)}), bf16[32,24,354]{2,1,0:T(8,128)(2,1)S(1)}, u32[]{:S(2)}, u32[]{:S(2)}) async-start(bf16[32,24,354]{2,1,0:T(8,128)(2,1)} %get-tuple-element.82), calls=%async_computation.1 | async-start | bytes 1179648 | tf_op jit(solution)/shard_map/all_to_all | solution.py:932
  62.2 6.6 %act_grads.1.grad_act_far = f32[354,3072]{1,0:T(8,128)} custom-call(bf16[354,768]{1,0:T(8,128)(2,1)} %get-tuple-element.153.scaled.scaled_far, bf16[3072,768]{1,0:T(8,128)(2,1)} %weight_far.3, f32[3,768]{1,0:T(4,128)} %pad_maximum_fusion.rest_0_.given_far), custom_call_target="tpu_custom_call" | custom-call | flops 1000 | bytes 22140000 | tf_op jit(solution)/shard_map/act_grads/pallas_call | solution.py:564
  70.6 6.5 %all-to-all-done.1.blocks = bf16[32,24,354]{2,1,0:T(8,128)(2,1)S(1)} async-done(((bf16[32,24,354]{2,1,0:T(8,128)(2,1)}), bf16[32,24,354]{2,1,0:T(8,128)(2,1)S(1)}, u32[]{:S(2)}, u32[]{:S(2)}) %all-to-all-start.1) | async-done | bytes 543776 | tf_op jit(solution)/shard_map/all_to_all | solution.py:932
  77.1 12.1 %feed_forward.1 = (bf16[32,24,354]{2,1,0:T(8,128)(2,1)}, bf16[354,3072]{1,0:T(8,128)(2,1)}, f32[768,128]{1,0:T(8,128)}, f32[1,3072]{1,0:T(1,128)}, bf16[3,16,32,...) custom-call(bf16[32,24,354]{2,1,0:T(8,128)(2,1)S(1)} %all-to-all-don, ...), custom_call_target="tpu_custom_call" | custom-call | flops 1000 | bytes 36900000 | tf_op jit(solution)/shard_map/feed_forward/pallas_call | solution.py:564
  89.3 3.5 %all-to-all-start.2 = ((bf16[32,24,354]{2,1,0:T(8,128)(2,1)}), bf16[32,24,354]{2,1,0:T(8,128)(2,1)S(1)}, u32[]{:S(2)}, u32[]{:S(2)}) async-start(bf16[32,24,354]{2,1,0:T(8,128)(2,1)} %get-tuple-element.83), calls=%async_computation.2 | async-start | bytes 1179648 | tf_op jit(solution)/shard_map/all_to_all | solution.py:932
  93.9 6.4 %out_grad_halves.1 = (bf16[3,16,32,768]{3,2,1,0:T(8,128)(2,1)}, bf16[3,4,32,768]{3,2,1,0:T(8,128)(2,1)}, bf16[3,4,32,768]{3,2,1,0:T(8,128)(2,1)}, bf16[3,4,32,768]{3,2,1,0:T(8,128)(2,1)}, bf16[3,4,32,768]{3,2,1,0:T(8,128)(2,1)}) custom-call(bf16[354,3072]{1,0:T(8,128)(2,1)} %get-tuple-element.84.act_far, bf16[354,768]{1,0:T(8,128)(2,1)} %get-tuple-element.153.scaled.scaled_far), custom_call_target="tpu_custom_call" | custom-call | flops 1000 | bytes 36900 | tf_op jit(solution)/shard_map/out_grad_halves/pallas_call | solution.py:564
  101.9 3.9 %collective-permute-done.5.refs_6_ = bf16[16,32,384]{2,1,0:T(8,128)(2,1)S(1)} collective-permute-done((bf16[16,32,384]{2,1,0:T(8,128)(2,1)}, bf16[16,32,384]{2,1,0:T(8,128)(2,1)S(1)}, u32[]{:S(2)}, u32[]{:S(2)}) %collective-permute-start.5) | collective-permute-done | bytes 393248 | tf_op jit(solution)/shard_map/ppermute | solution.py:962
  106.6 2.7 %all-to-all-done.2.refs_12_.block_far = bf16[32,24,354]{2,1,0:T(8,128)(2,1)S(1)} async-done(((bf16[32,24,354]{2,1,0:T(8,128)(2,1)}), bf16[32,24,354]{2,1,0:T(8,128)(2,1)S(1)}, u32[]{:S(2)}, u32[]{:S(2)}) %all-to-all-start.2) | async-done | bytes 543776 | tf_op jit(solution)/shard_map/all_to_all | solution.py:932
  110.1 4.2 %first_merge.1 = (bf16[8,64,768]{2,1,0:T(8,128)(2,1)S(1)}, bf16[8,64,768]{2,1,0:T(8,128)(2,1)S(1)}, bf16[8,64,768]{2,1,0:T(8,128)(2,1)S(1)}, bf16[8,64,768]{2,1,...) custom-call(bf16[3,16,32,768]{3,2,1,0:T(8,128)(2,1)} %get-tuple-element.87.r, ...), custom_call_target="tpu_custom_call" | custom-call | flops 1000 | bytes 36900 | tf_op jit(solution)/shard_map/first_merge/pallas_call | solution.py:564
  117.1 16.5 %mixer_arrive.1 = (f32[3312,128]{1,0:T(8,128)S(1)}, bf16[354,768]{1,0:T(8,128)(2,1)}, f32[768,128]{1,0:T(8,128)}, f32[8,128]{1,0:T(8,128)}) custom-call(s32[11328]{0:T(1024)} %select_select_fusion.where_far, bf16[32,24,354]{2,1,0:T(8,128)(2,1)} %copy-done, bf16[354,3072]{1,0:T(8,128)(2,1)} %get-tuple-element.84.act_far, bf16[3072,768]{1,0:T(8,128)(2,1)} %weight_far.3, ...), custom_call_target="tpu_custom_call" | custom-call | flops 1000 | bytes 36900 | tf_op jit(solution)/shard_map/mixer_arrive/pallas_call | solution.py:564
  139.6 8.0 %mixer_backward.1 = (f32[3312,128]{1,0:T(8,128)S(1)}, f32[336,128]{1,0:T(8,128)}, f32[336,128]{1,0:T(8,128)}, f32[8,128]{1,0:T(8,128)}, f32[8,128]{1,0:T(8,128)}) custom-call(f32[3312,128]{1,0:T(8,128)S(1)} %get-tuple-element.101.pg, f32[42,128]{1,0:T(8,128)} %pad.11.height_far.height, f32[42,128]{1,0:T(8,128)} %pad.12.width_far.width, ...), custom_call_target="tpu_custom_call" | custom-call | flops 1000 | bytes 36900 | tf_op jit(solution)/shard_map/mixer_backward/pallas_call | solution.py:564
  148.7 14.4 %mixer_leave.1 = (bf16[32,24,384]{2,1,0:T(8,128)(2,1)}, f32[8,128]{1,0:T(8,128)}) custom-call(s32[11328]{0:T(1024)} %select_select_fusion.where_far, f32[3312,128]{1,0:T(8,128)S(1)} %get-tuple-element.112.grads, f32[768,128]{1,0:T(8,128)} %get-tuple-element.113.extra, f32[8,128]{1,0:T(8,128)} %get-tuple-element.119.rest_0_), custom_call_target="tpu_custom_call" | custom-call | flops 1000 | bytes 36900 | tf_op jit(solution)/shard_map/mixer_leave/pallas_call | solution.py:564
  165.7 3.2 %all-to-all-start.3 = ((bf16[32,24,384]{2,1,0:T(8,128)(2,1)}), bf16[32,24,384]{2,1,0:T(8,128)(2,1)S(1)}, u32[]{:S(2)}, u32[]{:S(2)}) async-start(bf16[32,24,384]{2,1,0:T(8,128)(2,1)} %held_back.1), calls=%async_computation.3 | async-start | bytes 1179648 | tf_op jit(solution)/shard_map/all_to_all | solution.py:932
  168.9 1.8 collective-permute-start.17
  170.7 2.4 %collective-permute-start.18 = (bf16[1,128,768]{2,1,0:T(8,128)(2,1)}, bf16[1,128,768]{2,1,0:T(8,128)(2,1)}, u32[]{:S(2)}, u32[]{:S(2)}) collective-permute-start(bf16[1,128,768]{2,1,0:T(8,128)(2,1)} %get-tuple-element.142), channel_id=1, source_target_pairs={{0,16},{1,17},{2,18},{3,19},{4,20},{5,21},{6,22},{7,23},{8,24},{9,... | collective-permute-start | bytes 589832 | tf_op jit(solution)/shard_map/ppermute | solution.py:962
  173.1 8.2 %collective-permute-done.17.refs_1_ = bf16[2,64,768]{2,1,0:T(8,128)(2,1)S(1)} collective-permute-done((bf16[2,64,768]{2,1,0:T(8,128)(2,1)S(1)}, bf16[2,64,768]{2,1,0:T(8,128)(2,1)S(1)}, u32[]{:S(2)}, u32[]{:S(2)}) %collective-permute-start.17) | collective-permute-done | bytes 196640 | tf_op jit(solution)/shard_map/ppermute | solution.py:962
  183.3 2.4 %tap_grads.1 = (f32[24,64]{1,0:T(8,128)}, f32[24,64]{1,0:T(8,128)}, f32[24,64]{1,0:T(8,128)}, f32[24,64]{1,0:T(8,128)}, f32[1,24]{1,0:T(1,128)}) custom-call(f32[24,64]{1,0:T(8,128)} %coef_height.1, f32[24,64]{1,0:T(8,128)} %rate_height.1, f32[24,64]{1,0:T(8,128)} %coef_width.1, f32[24,64]{1,0:T(8,128)} %rate_width.1, f32[24,128]{1,0:T(8,128)} %constant.69.spread, ...), custom_call_target="tpu_custom_call" | custom-call | flops 1000000 | bytes 36900 | tf_op jit(solution)/shard_map/tap_grads/pallas_call | solution.py:441
  185.8 4.2 %all-to-all-done.3.blocks = bf16[32,24,384]{2,1,0:T(8,128)(2,1)S(1)} async-done(((bf16[32,24,384]{2,1,0:T(8,128)(2,1)}), bf16[32,24,384]{2,1,0:T(8,128)(2,1)S(1)}, u32[]{:S(2)}, u32[]{:S(2)}) %all-to-all-start.3) | async-done | bytes 589856 | tf_op jit(solution)/shard_map/all_to_all | solution.py:932
  190.0 2.5 %token_grads.1 = (f32[354,768]{1,0:T(8,128)}, f32[1,24]{1,0:T(1,128)}, f32[1,24]{1,0:T(1,128)}, f32[1,96]{1,0:T(1,128)}, f32[1,24]{1,0:T(1,128)}, /*index=5*/f32[1,24]{1,0:T(1,128)}) custom-call(bf16[32,24,384]{2,1,0:T(8,128)(2,1)S(1)} %all-to-all-done.3.blocks, bf16[354,768]{1,0:T(8,128)(2,1)} %out_grad.1), custom_call_target="tpu_custom_call" | custom-call | flops 1000 | bytes 36900 | tf_op jit(solution)/shard_map/token_grads/pallas_call | solution.py:564
  193.8 1.8 last_sums.1
  (95 shorter events, 26.9 us)
Async XLA Ops:
  2.9 24.0 %all-to-all-start = ((bf16[32,24,354]{2,1,0:T(8,128)(2,1)}), bf16[32,24,354]{2,1,0:T(8,128)(2,1)S(1)}, u32[]{:S(2)}, u32[]{:S(2)}) async-start(bf16[32,24,354]{2,1,0:T(8,128)(2,1)} %bitcast.1), calls=%async_computation | async-start | bytes 1179648 | tf_op jit(solution)/shard_map/all_to_all | solution.py:932
  57.1 20.0 %all-to-all-start.1 = ((bf16[32,24,354]{2,1,0:T(8,128)(2,1)}), bf16[32,24,354]{2,1,0:T(8,128)(2,1)S(1)}, u32[]{:S(2)}, u32[]{:S(2)}) async-start(bf16[32,24,354]{2,1,0:T(8,128)(2,1)} %get-tuple-element.82), calls=%async_computation.1 | async-start | bytes 1179648 | tf_op jit(solution)/shard_map/all_to_all | solution.py:932
  89.3 20.0 %all-to-all-start.2 = ((bf16[32,24,354]{2,1,0:T(8,128)(2,1)}), bf16[32,24,354]{2,1,0:T(8,128)(2,1)S(1)}, u32[]{:S(2)}, u32[]{:S(2)}) async-start(bf16[32,24,354]{2,1,0:T(8,128)(2,1)} %get-tuple-element.83), calls=%async_computation.2 | async-start | bytes 1179648 | tf_op jit(solution)/shard_map/all_to_all | solution.py:932
  92.8 7.6 %collective-permute-start = (bf16[16,32,384]{2,1,0:T(8,128)(2,1)}, bf16[16,32,384]{2,1,0:T(8,128)(2,1)S(1)}, u32[]{:S(2)}, u32[]{:S(2)}) collective-permute-start(bf16[16,32,384]{2,1,0:T(8,128)(2,1)} %get-tuple-element.88), channel_id=1, source_target_pairs={{0,1},{1,0},{2,3},{3,2},{4,5},{5,4},{6,7},{7,6},{8,9},{9,8},{10,11... | collective-permute-start | bytes 1179656 | tf_op jit(solution)/shard_map/ppermute | solution.py:962
  92.9 8.0 %collective-permute-start.1 = (bf16[16,32,384]{2,1,0:T(8,128)(2,1)}, bf16[16,32,384]{2,1,0:T(8,128)(2,1)}, u32[]{:S(2)}, u32[]{:S(2)}) collective-permute-start(bf16[16,32,384]{2,1,0:T(8,128)(2,1)} %get-tuple-element.89), channel_id=1, source_target_pairs={{0,1},{1,0},{2,3},{3,2},{4,5},{5,4},{6,7},{7,6},{8,9},{9,8},{10,11... | collective-permute-start | bytes 1179656 | tf_op jit(solution)/shard_map/ppermute | solution.py:962
  93.4 7.6 %collective-permute-start.2 = (bf16[16,32,384]{2,1,0:T(8,128)(2,1)}, bf16[16,32,384]{2,1,0:T(8,128)(2,1)}, u32[]{:S(2)}, u32[]{:S(2)}) collective-permute-start(bf16[16,32,384]{2,1,0:T(8,128)(2,1)} %get-tuple-element.90), channel_id=1, source_target_pairs={{0,1},{1,0},{2,3},{3,2},{4,5},{5,4},{6,7},{7,6},{8,9},{9,8},{10,11... | collective-permute-start | bytes 1179656 | tf_op jit(solution)/shard_map/ppermute | solution.py:962
  93.4 8.0 %collective-permute-start.3 = (bf16[16,32,384]{2,1,0:T(8,128)(2,1)}, bf16[16,32,384]{2,1,0:T(8,128)(2,1)}, u32[]{:S(2)}, u32[]{:S(2)}) collective-permute-start(bf16[16,32,384]{2,1,0:T(8,128)(2,1)} %get-tuple-element.91), channel_id=1, source_target_pairs={{0,1},{1,0},{2,3},{3,2},{4,5},{5,4},{6,7},{7,6},{8,9},{9,8},{10,11... | collective-permute-start | bytes 1179656 | tf_op jit(solution)/shard_map/ppermute | solution.py:962
  93.9 7.6 %collective-permute-start.4 = (bf16[16,32,384]{2,1,0:T(8,128)(2,1)}, bf16[16,32,384]{2,1,0:T(8,128)(2,1)}, u32[]{:S(2)}, u32[]{:S(2)}) collective-permute-start(bf16[16,32,384]{2,1,0:T(8,128)(2,1)} %get-tuple-element.92), channel_id=1, source_target_pairs={{0,1},{1,0},{2,3},{3,2},{4,5},{5,4},{6,7},{7,6},{8,9},{9,8},{10,11... | collective-permute-start | bytes 1179656 | tf_op jit(solution)/shard_map/ppermute | solution.py:962
  100.4 5.4 %collective-permute-start.6 = (bf16[3,4,32,768]{3,2,1,0:T(8,128)(2,1)}, bf16[3,4,32,768]{3,2,1,0:T(8,128)(2,1)S(1)}, u32[]{:S(2)}, u32[]{:S(2)}) collective-permute-start(bf16[3,4,32,768]{3,2,1,0:T(8,128)(2,1)} %get-tuple-element.95), channel_id=1, source_target_pairs={{0,1},{1,0},{2,3},{3,2},{4,5},{5,4},{6,7},{7,6},{8,9},{9,8},{10,11... | collective-permute-start | bytes 1769480 | tf_op jit(solution)/shard_map/ppermute | solution.py:962
  100.9 4.9 %collective-permute-start.7 = (bf16[3,4,32,768]{3,2,1,0:T(8,128)(2,1)}, bf16[3,4,32,768]{3,2,1,0:T(8,128)(2,1)S(1)}, u32[]{:S(2)}, u32[]{:S(2)}) collective-permute-start(bf16[3,4,32,768]{3,2,1,0:T(8,128)(2,1)} %get-tuple-element.96), channel_id=1, source_target_pairs={{0,1},{1,0},{2,3},{3,2},{4,5},{5,4},{6,7},{7,6},{8,9},{9,8},{10,11... | collective-permute-start | bytes 1769480 | tf_op jit(solution)/shard_map/ppermute | solution.py:962
  101.0 4.9 %collective-permute-start.8 = (bf16[3,4,32,768]{3,2,1,0:T(8,128)(2,1)}, bf16[3,4,32,768]{3,2,1,0:T(8,128)(2,1)S(1)}, u32[]{:S(2)}, u32[]{:S(2)}) collective-permute-start(bf16[3,4,32,768]{3,2,1,0:T(8,128)(2,1)} %get-tuple-element.97), channel_id=1, source_target_pairs={{0,1},{1,0},{2,3},{3,2},{4,5},{5,4},{6,7},{7,6},{8,9},{9,8},{10,11... | collective-permute-start | bytes 1769480 | tf_op jit(solution)/shard_map/ppermute | solution.py:962
  101.4 5.2 %collective-permute-start.9 = (bf16[3,4,32,768]{3,2,1,0:T(8,128)(2,1)}, bf16[3,4,32,768]{3,2,1,0:T(8,128)(2,1)S(1)}, u32[]{:S(2)}, u32[]{:S(2)}) collective-permute-start(bf16[3,4,32,768]{3,2,1,0:T(8,128)(2,1)} %get-tuple-element.98), channel_id=1, source_target_pairs={{0,1},{1,0},{2,3},{3,2},{4,5},{5,4},{6,7},{7,6},{8,9},{9,8},{10,11... | collective-permute-start | bytes 1769480 | tf_op jit(solution)/shard_map/ppermute | solution.py:962
  101.5 4.3 %collective-permute-start.5 = (bf16[16,32,384]{2,1,0:T(8,128)(2,1)}, bf16[16,32,384]{2,1,0:T(8,128)(2,1)S(1)}, u32[]{:S(2)}, u32[]{:S(2)}) collective-permute-start(bf16[16,32,384]{2,1,0:T(8,128)(2,1)} %get-tuple-element.93), channel_id=1, source_target_pairs={{0,1},{1,0},{2,3},{3,2},{4,5},{5,4},{6,7},{7,6},{8,9},{9,8},{10,11... | collective-permute-start | bytes 1179656 | tf_op jit(solution)/shard_map/ppermute | solution.py:962
  114.3 19.5 %collective-permute-start.10 = (bf16[8,64,768]{2,1,0:T(8,128)(2,1)S(1)}, bf16[8,64,768]{2,1,0:T(8,128)(2,1)S(1)}, u32[]{:S(2)}, u32[]{:S(2)}) collective-permute-start(bf16[8,64,768]{2,1,0:T(8,128)(2,1)S(1)} %get-tuple-element.107), channel_id=1, source_target_pairs={{0,2},{1,3},{2,0},{3,1},{4,6},{5,7},{6,4},{7,5},{8,10},{9,11},{10,... | collective-permute-start | bytes 2359304 | tf_op jit(solution)/shard_map/ppermute | solution.py:962
  115.5 19.5 %collective-permute-start.11 = (bf16[8,64,768]{2,1,0:T(8,128)(2,1)S(1)}, bf16[8,64,768]{2,1,0:T(8,128)(2,1)S(1)}, u32[]{:S(2)}, u32[]{:S(2)}) collective-permute-start(bf16[8,64,768]{2,1,0:T(8,128)(2,1)S(1)} %get-tuple-element.108), channel_id=1, source_target_pairs={{0,4},{1,5},{2,6},{3,7},{4,0},{5,1},{6,2},{7,3},{8,12},{9,13},{10,... | collective-permute-start | bytes 2359304 | tf_op jit(solution)/shard_map/ppermute | solution.py:962
  117.0 18.5 %collective-permute-start.12 = (bf16[8,64,768]{2,1,0:T(8,128)(2,1)S(1)}, bf16[8,64,768]{2,1,0:T(8,128)(2,1)S(1)}, u32[]{:S(2)}, u32[]{:S(2)}) collective-permute-start(bf16[8,64,768]{2,1,0:T(8,128)(2,1)S(1)} %get-tuple-element.109), channel_id=1, source_target_pairs={{0,8},{1,9},{2,10},{3,11},{4,12},{5,13},{6,14},{7,15},{8,0},{9,1},... | collective-permute-start | bytes 2359304 | tf_op jit(solution)/shard_map/ppermute | solution.py:962
  136.2 11.5 %collective-permute-start.13 = (bf16[4,64,768]{2,1,0:T(8,128)(2,1)S(1)}, bf16[4,64,768]{2,1,0:T(8,128)(2,1)S(1)}, u32[]{:S(2)}, u32[]{:S(2)}) collective-permute-start(bf16[4,64,768]{2,1,0:T(8,128)(2,1)S(1)} %get-tuple-element.116), channel_id=1, source_target_pairs={{0,4},{1,5},{2,6},{3,7},{4,0},{5,1},{6,2},{7,3},{8,12},{9,13},{10,... | collective-permute-start | bytes 1179656 | tf_op jit(solution)/shard_map/ppermute | solution.py:962
  137.5 10.2 %collective-permute-start.14 = (bf16[4,64,768]{2,1,0:T(8,128)(2,1)S(1)}, bf16[4,64,768]{2,1,0:T(8,128)(2,1)S(1)}, u32[]{:S(2)}, u32[]{:S(2)}) collective-permute-start(bf16[4,64,768]{2,1,0:T(8,128)(2,1)S(1)} %get-tuple-element.117), channel_id=1, source_target_pairs={{0,2},{1,3},{2,0},{3,1},{4,6},{5,7},{6,4},{7,5},{8,10},{9,11},{10,... | collective-permute-start | bytes 1179656 | tf_op jit(solution)/shard_map/ppermute | solution.py:962
  138.0 25.1 %collective-permute-start.16 = (bf16[4,64,768]{2,1,0:T(8,128)(2,1)S(1)}, bf16[4,64,768]{2,1,0:T(8,128)(2,1)S(1)}, u32[]{:S(2)}, u32[]{:S(2)}) collective-permute-start(bf16[4,64,768]{2,1,0:T(8,128)(2,1)S(1)} %get-tuple-element.124), channel_id=1, source_target_pairs={{0,16},{1,17},{2,18},{3,19},{4,20},{5,21},{6,22},{7,23},{8,24},{9,... | collective-permute-start | bytes 1179656 | tf_op jit(solution)/shard_map/ppermute | solution.py:962
  148.3 16.6 %collective-permute-start.15 = (bf16[2,128,768]{2,1,0:T(8,128)(2,1)S(1)}, bf16[2,128,768]{2,1,0:T(8,128)(2,1)S(1)}, u32[]{:S(2)}, u32[]{:S(2)}) collective-permute-start(bf16[2,128,768]{2,1,0:T(8,128)(2,1)S(1)} %get-tuple-element.123), channel_id=1, source_target_pairs={{0,8},{1,9},{2,10},{3,11},{4,12},{5,13},{6,14},{7,15},{8,0},{9,1},... | collective-permute-start | bytes 1179656 | tf_op jit(solution)/shard_map/ppermute | solution.py:962
  165.7 24.3 %all-to-all-start.3 = ((bf16[32,24,384]{2,1,0:T(8,128)(2,1)}), bf16[32,24,384]{2,1,0:T(8,128)(2,1)S(1)}, u32[]{:S(2)}, u32[]{:S(2)}) async-start(bf16[32,24,384]{2,1,0:T(8,128)(2,1)} %held_back.1), calls=%async_computation.3 | async-start | bytes 1179648 | tf_op jit(solution)/shard_map/all_to_all | solution.py:932
  168.9 12.4 %collective-permute-start.17 = (bf16[2,64,768]{2,1,0:T(8,128)(2,1)S(1)}, bf16[2,64,768]{2,1,0:T(8,128)(2,1)S(1)}, u32[]{:S(2)}, u32[]{:S(2)}) collective-permute-start(bf16[2,64,768]{2,1,0:T(8,128)(2,1)S(1)} %get-tuple-element.132), channel_id=1, source_target_pairs={{0,2},{1,3},{2,0},{3,1},{4,6},{5,7},{6,4},{7,5},{8,10},{9,11},{10,... | collective-permute-start | bytes 589832 | tf_op jit(solution)/shard_map/ppermute | solution.py:962
  170.7 23.1 %collective-permute-start.18 = (bf16[1,128,768]{2,1,0:T(8,128)(2,1)}, bf16[1,128,768]{2,1,0:T(8,128)(2,1)}, u32[]{:S(2)}, u32[]{:S(2)}) collective-permute-start(bf16[1,128,768]{2,1,0:T(8,128)(2,1)} %get-tuple-element.142), channel_id=1, source_target_pairs={{0,16},{1,17},{2,18},{3,19},{4,20},{5,21},{6,22},{7,23},{8,24},{9,... | collective-permute-start | bytes 589832 | tf_op jit(solution)/shard_map/ppermute | solution.py:962
  181.9 11.9 %collective-permute-start.19 = (bf16[1,64,768]{2,1,0:T(8,128)(2,1)S(1)}, bf16[1,64,768]{2,1,0:T(8,128)(2,1)}, u32[]{:S(2)}, u32[]{:S(2)}) collective-permute-start(bf16[1,64,768]{2,1,0:T(8,128)(2,1)S(1)} %get-tuple-element.144), channel_id=1, source_target_pairs={{0,4},{1,5},{2,6},{3,7},{4,0},{5,1},{6,2},{7,3},{8,12},{9,13},{10,... | collective-permute-start | bytes 294920 | tf_op jit(solution)/shard_map/ppermute | solution.py:962
  (16 other events, 256.0 us)
where the time goes:
time: 197 us; the launch traced here: 196 us
  Pallas kernels  108 us (55%)
  waiting for transfers between devices  43.7 us (22%)
  starting transfers between devices  32.5 us (16%)
  local copies, waits for them, and re-layouts  7.81 us (4%)
  other arithmetic  2.74 us (1%)
    pallas_call x14, Pallas kernels, run(): pl.pallas_call(kernel, out_shape=tuple((make[place](shape, dtype) for sha...  105 us
    all_to_all x4, waiting for transfers between devices, exchange(): return lax.all_to_all(blocks, 'chan', 0, 0, tiled=True)  26.6 us
    all_to_all x4, starting transfers between devices, exchange(): return lax.all_to_all(blocks, 'chan', 0, 0, tiled=True)  17.5 us
    ppermute x20, waiting for transfers between devices, swapped(): lax.ppermute(x, 'chan', [(i, i ^ 1 << bit) for i in range(lax.axis_size('...  17.1 us
    ppermute x20, starting transfers between devices, swapped(): lax.ppermute(x, 'chan', [(i, i ^ 1 << bit) for i in range(lax.axis_size('...  15 us
  transfers between devices with their start and end apart: 24, of which 11 were waited for; matrix products, arithmetic and copies ran while one was open for 3% of the time, Pallas kernels for 30%

commit v1 on v0

--- a/solution.py
+++ b/solution.py
@@ -320,12 +320,15 @@
     gather_rows(plan, where, (near, far), image, out, halves)
 
 
-def backward_kernel(plan, pg, height, width, skip, packed_far, across_far, *rest):
-    out, height_sums, width_sums, skip_sums, mark, pd, height_wide, width_wide, packed, across, sems = rest[-11:]
+def backward_kernel(plan, pg, height_far, width_far, skip_far, packed_far, across_far, *rest):
+    out, height_sums, width_sums, skip_sums, mark, pd, height_wide, width_wide, packed, across, sems, height, width, skip = rest[-14:]
+    small = started([(height_far, height), (width_far, width), (skip_far, skip)], sems.at[pl.ds(2, 3)])
     mark[...] = jnp.zeros_like(mark)
-    arriving = started([(across_far, across), (packed_far, packed)], sems)
+    arriving = started([(across_far, across), (packed_far, packed)], sems.at[pl.ds(0, 2)])
     place = lax.broadcasted_iota(jnp.int32, (SUB, LANES), 0)
     pd[pl.ds(plan.packed_rows, MARGIN), :] = jnp.zeros((MARGIN, LANES), F32)
+    for copy in small:
+        copy.wait()
     wide_taps(plan, height, height_wide)
     wide_taps(plan, width, width_wide)
     skips = jnp.broadcast_to(skip[...], (SUB, LANES))
@@ -480,10 +483,10 @@
 
 def mixer_backward(plan, grads, height, width, skip, packed, across, after):
     rows = plan.packed_rows
-    ins = [(grads, NEAR), (height, AUTO), (width, AUTO), (skip, AUTO), (packed, FAR), (across, FAR)]
+    ins = [(grads, NEAR)] + [(value, FAR) for value in (height, width, skip, packed, across)]
     outs = [((rows, LANES), F32, NEAR)] + [((size, LANES), F32, AUTO) for size in (TAPS * SUB, TAPS * SUB, SUB, SUB)]
     room = [pltpu.VMEM((size, LANES), F32) for size in (rows + MARGIN, TAPS * SUB, TAPS * SUB, rows, rows)]
-    room += [pltpu.SemaphoreType.DMA((2,))]
+    room += [pltpu.SemaphoreType.DMA((5,))] + [pltpu.VMEM(value.shape, F32) for value in (height, width, skip)]
     return run(functools.partial(backward_kernel, plan), "mixer_backward", ins, outs, room, after, limit=LESS)
 
 

time: 197 us -> 196 us (level)
  no operation moved by 1% of the time
where the time goes in v1:
time: 196 us
  Pallas kernels  108 us (55%)
  waiting for transfers between devices  43.7 us (22%)
  starting transfers between devices  32.6 us (17%)
  local copies, waits for them, and re-layouts  7.81 us (4%)
  other arithmetic  2.74 us (1%)
    pallas_call x14, Pallas kernels, run(): pl.pallas_call(kernel, out_shape=tuple((make[place](shape, dtype) for sha...  105 us
    all_to_all x4, waiting for transfers between devices, exchange(): return lax.all_to_all(blocks, 'chan', 0, 0, tiled=True)  26.7 us
    all_to_all x4, starting transfers between devices, exchange(): return lax.all_to_all(blocks, 'chan', 0, 0, tiled=True)  17.4 us
    ppermute x20, waiting for transfers between devices, swapped(): lax.ppermute(x, 'chan', [(i, i ^ 1 << bit) for i in range(lax.axis_size('...  17.1 us
    ppermute x20, starting transfers between devices, swapped(): lax.ppermute(x, 'chan', [(i, i ^ 1 << bit) for i in range(lax.axis_size('...  15.2 us
  transfers between devices with their start and end apart: 24, of which 11 were waited for; matrix products, arithmetic and copies ran while one was open for 3% of the time, Pallas kernels for 30%

profile of v1, /device:TPU:0, one launch (start us, length us, event | category | flops | bytes accessed | tf_op | source)
XLA Modules:
  0.0 195.5 jit_solution(13929765673160315446)
XLA Ops:
  0.7 2.1 %copy.48 = bf16[768,354]{1,0:T(8,128)(2,1)} copy(bf16[768,354]{0,1:T(8,128)(2,1)} %bitcast.11) | data formatting | bytes 1087488 | tf_op jit(solution)/shard_map/transpose | solution.py:939
  2.9 7.3 %all-to-all-start = ((bf16[32,24,354]{2,1,0:T(8,128)(2,1)}), bf16[32,24,354]{2,1,0:T(8,128)(2,1)S(1)}, u32[]{:S(2)}, u32[]{:S(2)}) async-start(bf16[32,24,354]{2,1,0:T(8,128)(2,1)} %bitcast.1), calls=%async_computation | async-start | bytes 1179648 | tf_op jit(solution)/shard_map/all_to_all | solution.py:935
  13.6 13.3 %all-to-all-done.block = bf16[32,24,354]{2,1,0:T(8,128)(2,1)S(1)} async-done(((bf16[32,24,354]{2,1,0:T(8,128)(2,1)}), bf16[32,24,354]{2,1,0:T(8,128)(2,1)S(1)}, u32[]{:S(2)}, u32[]{:S(2)}) %all-to-all-start) | async-done | bytes 543776 | tf_op jit(solution)/shard_map/all_to_all | solution.py:935
  26.9 30.2 %mixer_forward.1 = (bf16[32,24,354]{2,1,0:T(8,128)(2,1)}, f32[3312,128]{1,0:T(8,128)}, f32[3312,128]{1,0:T(8,128)}) custom-call(s32[11328]{0:T(1024)} %select_select_fusion.where_far, bf16[32,24,354]{2,1,0:T(8,128)(2,1)S(1)} %all-to-all-done.block, f32[42,128]{1,0:T(8,128)} %pad.11.height_far, f32[42,128]{1,0:T(8,128)} %pad.12.width_far, f32[1,128]{1,0:T(1,128)} %pad.13.skip_far), custom_call_target="tpu_custom_call" | custom-call | flops 1000 | bytes 110700000 | tf_op jit(solution)/shard_map/mixer_forward/pallas_call | solution.py:567
  57.1 3.5 %all-to-all-start.1 = ((bf16[32,24,354]{2,1,0:T(8,128)(2,1)}), bf16[32,24,354]{2,1,0:T(8,128)(2,1)S(1)}, u32[]{:S(2)}, u32[]{:S(2)}) async-start(bf16[32,24,354]{2,1,0:T(8,128)(2,1)} %get-tuple-element.82), calls=%async_computation.1 | async-start | bytes 1179648 | tf_op jit(solution)/shard_map/all_to_all | solution.py:935
  62.2 6.6 %act_grads.1.grad_act_far = f32[354,3072]{1,0:T(8,128)} custom-call(bf16[354,768]{1,0:T(8,128)(2,1)} %get-tuple-element.153.scaled.scaled_far, bf16[3072,768]{1,0:T(8,128)(2,1)} %weight_far.3, f32[3,768]{1,0:T(4,128)} %pad_maximum_fusion.rest_0_.given_far), custom_call_target="tpu_custom_call" | custom-call | flops 1000 | bytes 22140000 | tf_op jit(solution)/shard_map/act_grads/pallas_call | solution.py:567
  70.6 6.5 %all-to-all-done.1.blocks = bf16[32,24,354]{2,1,0:T(8,128)(2,1)S(1)} async-done(((bf16[32,24,354]{2,1,0:T(8,128)(2,1)}), bf16[32,24,354]{2,1,0:T(8,128)(2,1)S(1)}, u32[]{:S(2)}, u32[]{:S(2)}) %all-to-all-start.1) | async-done | bytes 543776 | tf_op jit(solution)/shard_map/all_to_all | solution.py:935
  77.1 12.1 %feed_forward.1 = (bf16[32,24,354]{2,1,0:T(8,128)(2,1)}, bf16[354,3072]{1,0:T(8,128)(2,1)}, f32[768,128]{1,0:T(8,128)}, f32[1,3072]{1,0:T(1,128)}, bf16[3,16,32,...) custom-call(bf16[32,24,354]{2,1,0:T(8,128)(2,1)S(1)} %all-to-all-don, ...), custom_call_target="tpu_custom_call" | custom-call | flops 1000 | bytes 36900000 | tf_op jit(solution)/shard_map/feed_forward/pallas_call | solution.py:567
  89.3 3.5 %all-to-all-start.2 = ((bf16[32,24,354]{2,1,0:T(8,128)(2,1)}), bf16[32,24,354]{2,1,0:T(8,128)(2,1)S(1)}, u32[]{:S(2)}, u32[]{:S(2)}) async-start(bf16[32,24,354]{2,1,0:T(8,128)(2,1)} %get-tuple-element.83), calls=%async_computation.2 | async-start | bytes 1179648 | tf_op jit(solution)/shard_map/all_to_all | solution.py:935
  93.9 6.4 %out_grad_halves.1 = (bf16[3,16,32,768]{3,2,1,0:T(8,128)(2,1)}, bf16[3,4,32,768]{3,2,1,0:T(8,128)(2,1)}, bf16[3,4,32,768]{3,2,1,0:T(8,128)(2,1)}, bf16[3,4,32,768]{3,2,1,0:T(8,128)(2,1)}, bf16[3,4,32,768]{3,2,1,0:T(8,128)(2,1)}) custom-call(bf16[354,3072]{1,0:T(8,128)(2,1)} %get-tuple-element.84.act_far, bf16[354,768]{1,0:T(8,128)(2,1)} %get-tuple-element.153.scaled.scaled_far), custom_call_target="tpu_custom_call" | custom-call | flops 1000 | bytes 36900 | tf_op jit(solution)/shard_map/out_grad_halves/pallas_call | solution.py:567
  101.9 3.9 %collective-permute-done.5.refs_6_ = bf16[16,32,384]{2,1,0:T(8,128)(2,1)S(1)} collective-permute-done((bf16[16,32,384]{2,1,0:T(8,128)(2,1)}, bf16[16,32,384]{2,1,0:T(8,128)(2,1)S(1)}, u32[]{:S(2)}, u32[]{:S(2)}) %collective-permute-start.5) | collective-permute-done | bytes 393248 | tf_op jit(solution)/shard_map/ppermute | solution.py:965
  106.6 2.7 %all-to-all-done.2.refs_12_.block_far = bf16[32,24,354]{2,1,0:T(8,128)(2,1)S(1)} async-done(((bf16[32,24,354]{2,1,0:T(8,128)(2,1)}), bf16[32,24,354]{2,1,0:T(8,128)(2,1)S(1)}, u32[]{:S(2)}, u32[]{:S(2)}) %all-to-all-start.2) | async-done | bytes 543776 | tf_op jit(solution)/shard_map/all_to_all | solution.py:935
  110.1 4.2 %first_merge.1 = (bf16[8,64,768]{2,1,0:T(8,128)(2,1)S(1)}, bf16[8,64,768]{2,1,0:T(8,128)(2,1)S(1)}, bf16[8,64,768]{2,1,0:T(8,128)(2,1)S(1)}, bf16[8,64,768]{2,1,...) custom-call(bf16[3,16,32,768]{3,2,1,0:T(8,128)(2,1)} %get-tuple-element.87.r, ...), custom_call_target="tpu_custom_call" | custom-call | flops 1000 | bytes 36900 | tf_op jit(solution)/shard_map/first_merge/pallas_call | solution.py:567
  117.2 16.5 %mixer_arrive.1 = (f32[3312,128]{1,0:T(8,128)S(1)}, bf16[354,768]{1,0:T(8,128)(2,1)}, f32[768,128]{1,0:T(8,128)}, f32[8,128]{1,0:T(8,128)}) custom-call(s32[11328]{0:T(1024)} %select_select_fusion.where_far, bf16[32,24,354]{2,1,0:T(8,128)(2,1)} %copy-done, bf16[354,3072]{1,0:T(8,128)(2,1)} %get-tuple-element.84.act_far, bf16[3072,768]{1,0:T(8,128)(2,1)} %weight_far.3, ...), custom_call_target="tpu_custom_call" | custom-call | flops 1000 | bytes 36900 | tf_op jit(solution)/shard_map/mixer_arrive/pallas_call | solution.py:567
  139.6 7.8 %mixer_backward.1 = (f32[3312,128]{1,0:T(8,128)S(1)}, f32[336,128]{1,0:T(8,128)}, f32[336,128]{1,0:T(8,128)}, f32[8,128]{1,0:T(8,128)}, f32[8,128]{1,0:T(8,128)}) custom-call(f32[3312,128]{1,0:T(8,128)S(1)} %get-tuple-element.101.pg, f32[42,128]{1,0:T(8,128)} %pad.11.height_far, f32[42,128]{1,0:T(8,128)} %pad.12.width_far, f32[1,128]{1,0:T(1,128)} %pad.13.skip_far, ...), custom_call_target="tpu_custom_call" | custom-call | flops 1000 | bytes 36900 | tf_op jit(solution)/shard_map/mixer_backward/pallas_call | solution.py:567
  148.7 14.4 %mixer_leave.1 = (bf16[32,24,384]{2,1,0:T(8,128)(2,1)}, f32[8,128]{1,0:T(8,128)}) custom-call(s32[11328]{0:T(1024)} %select_select_fusion.where_far, f32[3312,128]{1,0:T(8,128)S(1)} %get-tuple-element.112.grads, f32[768,128]{1,0:T(8,128)} %get-tuple-element.113.extra, f32[8,128]{1,0:T(8,128)} %get-tuple-element.119.rest_0_), custom_call_target="tpu_custom_call" | custom-call | flops 1000 | bytes 36900 | tf_op jit(solution)/shard_map/mixer_leave/pallas_call | solution.py:567
  165.7 3.1 %all-to-all-start.3 = ((bf16[32,24,384]{2,1,0:T(8,128)(2,1)}), bf16[32,24,384]{2,1,0:T(8,128)(2,1)S(1)}, u32[]{:S(2)}, u32[]{:S(2)}) async-start(bf16[32,24,384]{2,1,0:T(8,128)(2,1)} %held_back.1), calls=%async_computation.3 | async-start | bytes 1179648 | tf_op jit(solution)/shard_map/all_to_all | solution.py:935
  168.8 1.8 collective-permute-start.17
  170.6 2.4 %collective-permute-start.18 = (bf16[1,128,768]{2,1,0:T(8,128)(2,1)}, bf16[1,128,768]{2,1,0:T(8,128)(2,1)}, u32[]{:S(2)}, u32[]{:S(2)}) collective-permute-start(bf16[1,128,768]{2,1,0:T(8,128)(2,1)} %get-tuple-element.142), channel_id=1, source_target_pairs={{0,16},{1,17},{2,18},{3,19},{4,20},{5,21},{6,22},{7,23},{8,24},{9,... | collective-permute-start | bytes 589832 | tf_op jit(solution)/shard_map/ppermute | solution.py:965
  173.0 8.2 %collective-permute-done.17.refs_1_ = bf16[2,64,768]{2,1,0:T(8,128)(2,1)S(1)} collective-permute-done((bf16[2,64,768]{2,1,0:T(8,128)(2,1)S(1)}, bf16[2,64,768]{2,1,0:T(8,128)(2,1)S(1)}, u32[]{:S(2)}, u32[]{:S(2)}) %collective-permute-start.17) | collective-permute-done | bytes 196640 | tf_op jit(solution)/shard_map/ppermute | solution.py:965
  183.2 2.4 %tap_grads.1 = (f32[24,64]{1,0:T(8,128)}, f32[24,64]{1,0:T(8,128)}, f32[24,64]{1,0:T(8,128)}, f32[24,64]{1,0:T(8,128)}, f32[1,24]{1,0:T(1,128)}) custom-call(f32[24,64]{1,0:T(8,128)} %coef_height.1, f32[24,64]{1,0:T(8,128)} %rate_height.1, f32[24,64]{1,0:T(8,128)} %coef_width.1, f32[24,64]{1,0:T(8,128)} %rate_width.1, f32[24,128]{1,0:T(8,128)} %constant.69.spread, ...), custom_call_target="tpu_custom_call" | custom-call | flops 1000000 | bytes 36900 | tf_op jit(solution)/shard_map/tap_grads/pallas_call | solution.py:444
  185.7 4.2 %all-to-all-done.3.blocks = bf16[32,24,384]{2,1,0:T(8,128)(2,1)S(1)} async-done(((bf16[32,24,384]{2,1,0:T(8,128)(2,1)}), bf16[32,24,384]{2,1,0:T(8,128)(2,1)S(1)}, u32[]{:S(2)}, u32[]{:S(2)}) %all-to-all-start.3) | async-done | bytes 589856 | tf_op jit(solution)/shard_map/all_to_all | solution.py:935
  189.9 2.5 %token_grads.1 = (f32[354,768]{1,0:T(8,128)}, f32[1,24]{1,0:T(1,128)}, f32[1,24]{1,0:T(1,128)}, f32[1,96]{1,0:T(1,128)}, f32[1,24]{1,0:T(1,128)}, /*index=5*/f32[1,24]{1,0:T(1,128)}) custom-call(bf16[32,24,384]{2,1,0:T(8,128)(2,1)S(1)} %all-to-all-done.3.blocks, bf16[354,768]{1,0:T(8,128)(2,1)} %out_grad.1), custom_call_target="tpu_custom_call" | custom-call | flops 1000 | bytes 36900 | tf_op jit(solution)/shard_map/token_grads/pallas_call | solution.py:567
  193.7 1.8 last_sums.1
  (95 shorter events, 27.1 us)
Async XLA Ops:
  2.9 24.0 %all-to-all-start = ((bf16[32,24,354]{2,1,0:T(8,128)(2,1)}), bf16[32,24,354]{2,1,0:T(8,128)(2,1)S(1)}, u32[]{:S(2)}, u32[]{:S(2)}) async-start(bf16[32,24,354]{2,1,0:T(8,128)(2,1)} %bitcast.1), calls=%async_computation | async-start | bytes 1179648 | tf_op jit(solution)/shard_map/all_to_all | solution.py:935
  57.1 20.0 %all-to-all-start.1 = ((bf16[32,24,354]{2,1,0:T(8,128)(2,1)}), bf16[32,24,354]{2,1,0:T(8,128)(2,1)S(1)}, u32[]{:S(2)}, u32[]{:S(2)}) async-start(bf16[32,24,354]{2,1,0:T(8,128)(2,1)} %get-tuple-element.82), calls=%async_computation.1 | async-start | bytes 1179648 | tf_op jit(solution)/shard_map/all_to_all | solution.py:935
  89.3 20.0 %all-to-all-start.2 = ((bf16[32,24,354]{2,1,0:T(8,128)(2,1)}), bf16[32,24,354]{2,1,0:T(8,128)(2,1)S(1)}, u32[]{:S(2)}, u32[]{:S(2)}) async-start(bf16[32,24,354]{2,1,0:T(8,128)(2,1)} %get-tuple-element.83), calls=%async_computation.2 | async-start | bytes 1179648 | tf_op jit(solution)/shard_map/all_to_all | solution.py:935
  92.8 7.6 %collective-permute-start = (bf16[16,32,384]{2,1,0:T(8,128)(2,1)}, bf16[16,32,384]{2,1,0:T(8,128)(2,1)S(1)}, u32[]{:S(2)}, u32[]{:S(2)}) collective-permute-start(bf16[16,32,384]{2,1,0:T(8,128)(2,1)} %get-tuple-element.88), channel_id=1, source_target_pairs={{0,1},{1,0},{2,3},{3,2},{4,5},{5,4},{6,7},{7,6},{8,9},{9,8},{10,11... | collective-permute-start | bytes 1179656 | tf_op jit(solution)/shard_map/ppermute | solution.py:965
  92.9 8.0 %collective-permute-start.1 = (bf16[16,32,384]{2,1,0:T(8,128)(2,1)}, bf16[16,32,384]{2,1,0:T(8,128)(2,1)}, u32[]{:S(2)}, u32[]{:S(2)}) collective-permute-start(bf16[16,32,384]{2,1,0:T(8,128)(2,1)} %get-tuple-element.89), channel_id=1, source_target_pairs={{0,1},{1,0},{2,3},{3,2},{4,5},{5,4},{6,7},{7,6},{8,9},{9,8},{10,11... | collective-permute-start | bytes 1179656 | tf_op jit(solution)/shard_map/ppermute | solution.py:965
  93.4 7.6 %collective-permute-start.2 = (bf16[16,32,384]{2,1,0:T(8,128)(2,1)}, bf16[16,32,384]{2,1,0:T(8,128)(2,1)}, u32[]{:S(2)}, u32[]{:S(2)}) collective-permute-start(bf16[16,32,384]{2,1,0:T(8,128)(2,1)} %get-tuple-element.90), channel_id=1, source_target_pairs={{0,1},{1,0},{2,3},{3,2},{4,5},{5,4},{6,7},{7,6},{8,9},{9,8},{10,11... | collective-permute-start | bytes 1179656 | tf_op jit(solution)/shard_map/ppermute | solution.py:965
  93.4 8.0 %collective-permute-start.3 = (bf16[16,32,384]{2,1,0:T(8,128)(2,1)}, bf16[16,32,384]{2,1,0:T(8,128)(2,1)}, u32[]{:S(2)}, u32[]{:S(2)}) collective-permute-start(bf16[16,32,384]{2,1,0:T(8,128)(2,1)} %get-tuple-element.91), channel_id=1, source_target_pairs={{0,1},{1,0},{2,3},{3,2},{4,5},{5,4},{6,7},{7,6},{8,9},{9,8},{10,11... | collective-permute-start | bytes 1179656 | tf_op jit(solution)/shard_map/ppermute | solution.py:965
  93.9 7.6 %collective-permute-start.4 = (bf16[16,32,384]{2,1,0:T(8,128)(2,1)}, bf16[16,32,384]{2,1,0:T(8,128)(2,1)}, u32[]{:S(2)}, u32[]{:S(2)}) collective-permute-start(bf16[16,32,384]{2,1,0:T(8,128)(2,1)} %get-tuple-element.92), channel_id=1, source_target_pairs={{0,1},{1,0},{2,3},{3,2},{4,5},{5,4},{6,7},{7,6},{8,9},{9,8},{10,11... | collective-permute-start | bytes 1179656 | tf_op jit(solution)/shard_map/ppermute | solution.py:965
  100.4 5.4 %collective-permute-start.6 = (bf16[3,4,32,768]{3,2,1,0:T(8,128)(2,1)}, bf16[3,4,32,768]{3,2,1,0:T(8,128)(2,1)S(1)}, u32[]{:S(2)}, u32[]{:S(2)}) collective-permute-start(bf16[3,4,32,768]{3,2,1,0:T(8,128)(2,1)} %get-tuple-element.95), channel_id=1, source_target_pairs={{0,1},{1,0},{2,3},{3,2},{4,5},{5,4},{6,7},{7,6},{8,9},{9,8},{10,11... | collective-permute-start | bytes 1769480 | tf_op jit(solution)/shard_map/ppermute | solution.py:965
  100.9 4.9 %collective-permute-start.7 = (bf16[3,4,32,768]{3,2,1,0:T(8,128)(2,1)}, bf16[3,4,32,768]{3,2,1,0:T(8,128)(2,1)S(1)}, u32[]{:S(2)}, u32[]{:S(2)}) collective-permute-start(bf16[3,4,32,768]{3,2,1,0:T(8,128)(2,1)} %get-tuple-element.96), channel_id=1, source_target_pairs={{0,1},{1,0},{2,3},{3,2},{4,5},{5,4},{6,7},{7,6},{8,9},{9,8},{10,11... | collective-permute-start | bytes 1769480 | tf_op jit(solution)/shard_map/ppermute | solution.py:965
  101.0 4.9 %collective-permute-start.8 = (bf16[3,4,32,768]{3,2,1,0:T(8,128)(2,1)}, bf16[3,4,32,768]{3,2,1,0:T(8,128)(2,1)S(1)}, u32[]{:S(2)}, u32[]{:S(2)}) collective-permute-start(bf16[3,4,32,768]{3,2,1,0:T(8,128)(2,1)} %get-tuple-element.97), channel_id=1, source_target_pairs={{0,1},{1,0},{2,3},{3,2},{4,5},{5,4},{6,7},{7,6},{8,9},{9,8},{10,11... | collective-permute-start | bytes 1769480 | tf_op jit(solution)/shard_map/ppermute | solution.py:965
  101.4 5.2 %collective-permute-start.9 = (bf16[3,4,32,768]{3,2,1,0:T(8,128)(2,1)}, bf16[3,4,32,768]{3,2,1,0:T(8,128)(2,1)S(1)}, u32[]{:S(2)}, u32[]{:S(2)}) collective-permute-start(bf16[3,4,32,768]{3,2,1,0:T(8,128)(2,1)} %get-tuple-element.98), channel_id=1, source_target_pairs={{0,1},{1,0},{2,3},{3,2},{4,5},{5,4},{6,7},{7,6},{8,9},{9,8},{10,11... | collective-permute-start | bytes 1769480 | tf_op jit(solution)/shard_map/ppermute | solution.py:965
  101.5 4.3 %collective-permute-start.5 = (bf16[16,32,384]{2,1,0:T(8,128)(2,1)}, bf16[16,32,384]{2,1,0:T(8,128)(2,1)S(1)}, u32[]{:S(2)}, u32[]{:S(2)}) collective-permute-start(bf16[16,32,384]{2,1,0:T(8,128)(2,1)} %get-tuple-element.93), channel_id=1, source_target_pairs={{0,1},{1,0},{2,3},{3,2},{4,5},{5,4},{6,7},{7,6},{8,9},{9,8},{10,11... | collective-permute-start | bytes 1179656 | tf_op jit(solution)/shard_map/ppermute | solution.py:965
  114.3 19.5 %collective-permute-start.10 = (bf16[8,64,768]{2,1,0:T(8,128)(2,1)S(1)}, bf16[8,64,768]{2,1,0:T(8,128)(2,1)S(1)}, u32[]{:S(2)}, u32[]{:S(2)}) collective-permute-start(bf16[8,64,768]{2,1,0:T(8,128)(2,1)S(1)} %get-tuple-element.107), channel_id=1, source_target_pairs={{0,2},{1,3},{2,0},{3,1},{4,6},{5,7},{6,4},{7,5},{8,10},{9,11},{10,... | collective-permute-start | bytes 2359304 | tf_op jit(solution)/shard_map/ppermute | solution.py:965
  115.5 19.5 %collective-permute-start.11 = (bf16[8,64,768]{2,1,0:T(8,128)(2,1)S(1)}, bf16[8,64,768]{2,1,0:T(8,128)(2,1)S(1)}, u32[]{:S(2)}, u32[]{:S(2)}) collective-permute-start(bf16[8,64,768]{2,1,0:T(8,128)(2,1)S(1)} %get-tuple-element.108), channel_id=1, source_target_pairs={{0,4},{1,5},{2,6},{3,7},{4,0},{5,1},{6,2},{7,3},{8,12},{9,13},{10,... | collective-permute-start | bytes 2359304 | tf_op jit(solution)/shard_map/ppermute | solution.py:965
  117.0 18.5 %collective-permute-start.12 = (bf16[8,64,768]{2,1,0:T(8,128)(2,1)S(1)}, bf16[8,64,768]{2,1,0:T(8,128)(2,1)S(1)}, u32[]{:S(2)}, u32[]{:S(2)}) collective-permute-start(bf16[8,64,768]{2,1,0:T(8,128)(2,1)S(1)} %get-tuple-element.109), channel_id=1, source_target_pairs={{0,8},{1,9},{2,10},{3,11},{4,12},{5,13},{6,14},{7,15},{8,0},{9,1},... | collective-permute-start | bytes 2359304 | tf_op jit(solution)/shard_map/ppermute | solution.py:965
  136.2 11.2 %collective-permute-start.13 = (bf16[4,64,768]{2,1,0:T(8,128)(2,1)S(1)}, bf16[4,64,768]{2,1,0:T(8,128)(2,1)S(1)}, u32[]{:S(2)}, u32[]{:S(2)}) collective-permute-start(bf16[4,64,768]{2,1,0:T(8,128)(2,1)S(1)} %get-tuple-element.116), channel_id=1, source_target_pairs={{0,4},{1,5},{2,6},{3,7},{4,0},{5,1},{6,2},{7,3},{8,12},{9,13},{10,... | collective-permute-start | bytes 1179656 | tf_op jit(solution)/shard_map/ppermute | solution.py:965
  137.5 10.0 %collective-permute-start.14 = (bf16[4,64,768]{2,1,0:T(8,128)(2,1)S(1)}, bf16[4,64,768]{2,1,0:T(8,128)(2,1)S(1)}, u32[]{:S(2)}, u32[]{:S(2)}) collective-permute-start(bf16[4,64,768]{2,1,0:T(8,128)(2,1)S(1)} %get-tuple-element.117), channel_id=1, source_target_pairs={{0,2},{1,3},{2,0},{3,1},{4,6},{5,7},{6,4},{7,5},{8,10},{9,11},{10,... | collective-permute-start | bytes 1179656 | tf_op jit(solution)/shard_map/ppermute | solution.py:965
  138.0 25.1 %collective-permute-start.16 = (bf16[4,64,768]{2,1,0:T(8,128)(2,1)S(1)}, bf16[4,64,768]{2,1,0:T(8,128)(2,1)S(1)}, u32[]{:S(2)}, u32[]{:S(2)}) collective-permute-start(bf16[4,64,768]{2,1,0:T(8,128)(2,1)S(1)} %get-tuple-element.124), channel_id=1, source_target_pairs={{0,16},{1,17},{2,18},{3,19},{4,20},{5,21},{6,22},{7,23},{8,24},{9,... | collective-permute-start | bytes 1179656 | tf_op jit(solution)/shard_map/ppermute | solution.py:965
  148.1 16.8 %collective-permute-start.15 = (bf16[2,128,768]{2,1,0:T(8,128)(2,1)S(1)}, bf16[2,128,768]{2,1,0:T(8,128)(2,1)S(1)}, u32[]{:S(2)}, u32[]{:S(2)}) collective-permute-start(bf16[2,128,768]{2,1,0:T(8,128)(2,1)S(1)} %get-tuple-element.123), channel_id=1, source_target_pairs={{0,8},{1,9},{2,10},{3,11},{4,12},{5,13},{6,14},{7,15},{8,0},{9,1},... | collective-permute-start | bytes 1179656 | tf_op jit(solution)/shard_map/ppermute | solution.py:965
  165.7 24.2 %all-to-all-start.3 = ((bf16[32,24,384]{2,1,0:T(8,128)(2,1)}), bf16[32,24,384]{2,1,0:T(8,128)(2,1)S(1)}, u32[]{:S(2)}, u32[]{:S(2)}) async-start(bf16[32,24,384]{2,1,0:T(8,128)(2,1)} %held_back.1), calls=%async_computation.3 | async-start | bytes 1179648 | tf_op jit(solution)/shard_map/all_to_all | solution.py:935
  168.8 12.4 %collective-permute-start.17 = (bf16[2,64,768]{2,1,0:T(8,128)(2,1)S(1)}, bf16[2,64,768]{2,1,0:T(8,128)(2,1)S(1)}, u32[]{:S(2)}, u32[]{:S(2)}) collective-permute-start(bf16[2,64,768]{2,1,0:T(8,128)(2,1)S(1)} %get-tuple-element.132), channel_id=1, source_target_pairs={{0,2},{1,3},{2,0},{3,1},{4,6},{5,7},{6,4},{7,5},{8,10},{9,11},{10,... | collective-permute-start | bytes 589832 | tf_op jit(solution)/shard_map/ppermute | solution.py:965
  170.6 23.1 %collective-permute-start.18 = (bf16[1,128,768]{2,1,0:T(8,128)(2,1)}, bf16[1,128,768]{2,1,0:T(8,128)(2,1)}, u32[]{:S(2)}, u32[]{:S(2)}) collective-permute-start(bf16[1,128,768]{2,1,0:T(8,128)(2,1)} %get-tuple-element.142), channel_id=1, source_target_pairs={{0,16},{1,17},{2,18},{3,19},{4,20},{5,21},{6,22},{7,23},{8,24},{9,... | collective-permute-start | bytes 589832 | tf_op jit(solution)/shard_map/ppermute | solution.py:965
  181.8 11.9 %collective-permute-start.19 = (bf16[1,64,768]{2,1,0:T(8,128)(2,1)S(1)}, bf16[1,64,768]{2,1,0:T(8,128)(2,1)}, u32[]{:S(2)}, u32[]{:S(2)}) collective-permute-start(bf16[1,64,768]{2,1,0:T(8,128)(2,1)S(1)} %get-tuple-element.144), channel_id=1, source_target_pairs={{0,4},{1,5},{2,6},{3,7},{4,0},{5,1},{6,2},{7,3},{8,12},{9,13},{10,... | collective-permute-start | bytes 294920 | tf_op jit(solution)/shard_map/ppermute | solution.py:965
  (16 other events, 256.0 us)
